TPU v7x, 32 devices: a whole 2x2x4 slice. The times are simulated.
32 devices in a mesh: section: 2 (over core), seq: 4 (over y, x), heads: 4 (over z).
Axes of the slice: x: 2, y: 2, z: 4, core: 2. Of those that a mesh axis runs over, the one named last changes fastest.
Arguments:
- frames: bfloat16 [2, 704, 1024], P(None, 'seq', 'heads'), may hold values from -6 to 6
- cotangent: bfloat16 [2, 704, 1024], P(None, 'seq', 'heads'), may hold values from -6 to 6
- utt_lengths: int32 [2, 3], replicated, may hold values from 1 to 702, as said below
- time_ids: int32 [2, 3], replicated, may hold values from 0 to 999
- w_time_in: bfloat16 [256, 1024], replicated, may hold values from -0.375 to 0.375
- w_time_out: bfloat16 [1024, 1024], replicated, may hold values from -0.1875 to 0.1875
- w_mod: bfloat16 [2, 1024, 6, 1024], P('section', None, None, 'heads'), may hold values from -0.375 to 0.375
- w_qkv: bfloat16 [2, 1024, 3, 1024], P('section', None, None, 'heads'), may hold values from -0.1875 to 0.1875
- w_out: bfloat16 [2, 1024, 1024], P('section', 'heads'), may hold values from -3 to 3
- w_up: bfloat16 [2, 1024, 2048], P('section', None, 'heads'), may hold values from -0.1875 to 0.1875
- w_down: bfloat16 [2, 2048, 1024], P('section', 'heads'), may hold values from -0.125 to 0.125
Outputs:
- acts: bfloat16 [2, 2, 704, 1024], P('section', None, 'seq', 'heads')
- grads: float32 [2, 2, 704, 1024], P('section', None, 'seq', 'heads')
- g_time_in: float32 [256, 1024], replicated
- g_time_out: float32 [1024, 1024], replicated
- g_mod: float32 [2, 1024, 6, 1024], P('section', None, None, 'heads')
- g_qkv: float32 [2, 1024, 3, 1024], P('section', None, None, 'heads')
- g_out: float32 [2, 1024, 1024], P('section', 'heads')
- g_up: float32 [2, 1024, 2048], P('section', None, 'heads')
- g_down: float32 [2, 2048, 1024], P('section', 'heads')
Inputs may be any that keep to these rules, and one draw needn't show every extreme that they name: `utt_lengths`: each micro-batch packs three utterances in order: the first and the last have 1 to 88 frames each, the middle one has the rest, so that the three sum to 704.
All inputs are finite; a program needn't handle non-finite values.
Results may differ from a plain program's by a relative error of at most 0.025.
Values may be sent and summed in bfloat16 or wider, within the bound.
No kernel may reach another device: no remote copies, remote signals or barrier semaphores. Data moves between devices by JAX's collectives and lax.ppermute only.
A program may use at most 128 MiB of HBM per device.

v0:
```python
import math

import jax
import jax.numpy as jnp
from jax import lax
from jax.sharding import PartitionSpec as P

HEAD_DIM = 64
FREQ = 256


def passed_along(value, axis, by):
    length = lax.axis_size(axis)
    pairs = [(i, i + by) for i in range(length) if 0 <= i + by < length]
    return lax.ppermute(value, axis, pairs)


def exact(spec, left, right):
    return jnp.einsum(spec, left, right, precision=lax.Precision.HIGHEST)


def sinusoid(time_ids):
    half_width = FREQ // 2
    frequency = jnp.exp(
        jnp.arange(half_width, dtype=jnp.float32) * (-math.log(10000.0) / (half_width - 1))
    )
    angle_t = time_ids.astype(jnp.float32)[..., None] * frequency
    return jnp.concatenate([jnp.sin(angle_t), jnp.cos(angle_t)], axis=-1)


def frame_layout(lengths, first_row, row_count):
    index_row = first_row + jnp.arange(row_count, dtype=jnp.int32)
    end_first = lengths[0]
    end_second = lengths[0] + lengths[1]
    segment = (index_row >= end_first).astype(jnp.int32) + (index_row >= end_second).astype(
        jnp.int32
    )
    begin_row = jnp.where(segment == 0, 0, jnp.where(segment == 1, end_first, end_second))
    position = (index_row - begin_row).astype(jnp.float32)
    one_hot_mask = (segment[:, None] == jnp.arange(3, dtype=jnp.int32)[None, :]).astype(jnp.float32)
    return (segment, position, one_hot_mask)


def segment_of(lengths, row_count):
    index_row = jnp.arange(row_count, dtype=jnp.int32)
    return (index_row >= lengths[0]).astype(jnp.int32) + (
        index_row >= lengths[0] + lengths[1]
    ).astype(jnp.int32)


def rotation(position):
    half_width = HEAD_DIM // 2
    rate_table = jnp.exp(
        jnp.arange(half_width, dtype=jnp.float32) * (-2.0 * math.log(10000.0) / HEAD_DIM)
    )
    angle_t = position[:, None] * rate_table[None, :]
    return (jnp.cos(angle_t)[:, None, :], jnp.sin(angle_t)[:, None, :])


def rotate(values_in, cosine_table, sine_timestep, sign_factor):
    paired = values_in.reshape(values_in.shape[:-1] + (HEAD_DIM // 2, 2))
    even_part = paired[..., 0]
    odd_part = paired[..., 1]
    turned_even = even_part * cosine_table - sign_factor * odd_part * sine_timestep
    turned_odd = sign_factor * even_part * sine_timestep + odd_part * cosine_table
    return jnp.stack([turned_even, turned_odd], axis=-1).reshape(values_in.shape)


def across_heads(first_sum, second_sum):
    return lax.psum((first_sum, second_sum), "heads")


def normalize(residual_input):
    full_width = residual_input.shape[1] * lax.axis_size("heads")
    row_total, square = across_heads(
        jnp.sum(residual_input, axis=1), jnp.sum(residual_input * residual_input, axis=1)
    )
    row_mean = row_total / full_width
    inv_std = lax.rsqrt(square / full_width - row_mean * row_mean + 1e-06)
    return ((residual_input - row_mean[:, None]) * inv_std[:, None], inv_std)


def norm_back(grad_norm, normed, inv_std):
    full_width = normed.shape[1] * lax.axis_size("heads")
    grad_total, cross_sum = across_heads(
        jnp.sum(grad_norm, axis=1), jnp.sum(grad_norm * normed, axis=1)
    )
    return inv_std[:, None] * (
        grad_norm - grad_total[:, None] / full_width - normed * (cross_sum / full_width)[:, None]
    )


def widen(narrow_part):
    return lax.all_gather(narrow_part, "heads", axis=1, tiled=True)


def reduce_heads(term):
    return lax.psum_scatter(
        term.astype(jnp.bfloat16), "heads", scatter_dimension=1, tiled=True
    ).astype(jnp.float32)


def widen_grad(narrow_part):
    return lax.all_gather(narrow_part, "heads", axis=1, tiled=True)


def sum_back(term):
    return lax.psum_scatter(
        term.astype(jnp.bfloat16), "heads", scatter_dimension=1, tiled=True
    ).astype(jnp.float32)


def block_scores(queries, key_block, seg_query, lengths):
    scores = jnp.einsum(
        "qhd,khd->hqk", queries, key_block, preferred_element_type=jnp.float32
    ) / math.sqrt(HEAD_DIM)
    same_utterance_mask = seg_query[:, None] == segment_of(lengths, key_block.shape[0])[None, :]
    return (scores, same_utterance_mask[None])


def attend(queries, key_block, value_block, seg_query, lengths):
    row_count, heads_here = (queries.shape[0], queries.shape[1])
    run_peak = jnp.full((heads_here, row_count), -1e30, jnp.float32)
    scores, same_utterance_mask = block_scores(
        queries, lax.all_gather(key_block, "seq", axis=0, tiled=True), seg_query, lengths
    )
    scores = jnp.where(same_utterance_mask, scores, -1e30)
    new_peak = jnp.maximum(run_peak, jnp.max(scores, axis=2))
    weights = jnp.where(same_utterance_mask, jnp.exp(scores - new_peak[:, :, None]), 0.0)
    run_total = jnp.sum(weights, axis=2)
    run_acc = jnp.einsum(
        "hqk,khd->hqd",
        weights.astype(jnp.bfloat16),
        lax.all_gather(value_block, "seq", axis=0, tiled=True),
        preferred_element_type=jnp.float32,
    )
    run_peak, run_total, run_acc = (new_peak, run_total, run_acc)
    mixed_heads = jnp.transpose(run_acc / run_total[:, :, None], (1, 0, 2))
    return (mixed_heads, run_peak + jnp.log(run_total))


def block_back(queries, grad_att, log_total, row_delta, seg_query, lengths, key_block, value_block):
    scores, same_utterance_mask = block_scores(queries, key_block, seg_query, lengths)
    probs_block = jnp.where(same_utterance_mask, jnp.exp(scores - log_total[:, :, None]), 0.0)
    grad_prob = jnp.einsum(
        "qhd,khd->hqk", grad_att, value_block, preferred_element_type=jnp.float32
    )
    grad_score = (probs_block * (grad_prob - row_delta[:, :, None])).astype(jnp.bfloat16)
    score_scale = 1.0 / math.sqrt(HEAD_DIM)
    grad_query = (
        jnp.einsum("hqk,khd->qhd", grad_score, key_block, preferred_element_type=jnp.float32)
        * score_scale
    )
    grad_key = (
        jnp.einsum("hqk,qhd->khd", grad_score, queries, preferred_element_type=jnp.float32)
        * score_scale
    )
    grad_value = jnp.einsum(
        "hqk,qhd->khd",
        probs_block.astype(jnp.bfloat16),
        grad_att,
        preferred_element_type=jnp.float32,
    )
    return (grad_query, grad_key, grad_value)


def layer_forward(
    residual_input,
    modulation_vector,
    one_hot_mask,
    cosine_table,
    sine_timestep,
    seg_query,
    lengths,
    weights,
):
    w_proj, w_project_out, w_expand, w_reduce = weights
    row_count = residual_input.shape[0]
    modulators = [
        exact("tu,ud->td", one_hot_mask, modulation_vector[:, which, :]) for which in range(6)
    ]
    normed_a, inv_std_a = normalize(residual_input)
    wide_a = widen((normed_a * (1.0 + modulators[1]) + modulators[0]).astype(jnp.bfloat16))
    projected = jnp.einsum("td,dce->tce", wide_a, w_proj, preferred_element_type=jnp.float32)
    shape_heads = (row_count, projected.shape[2] // HEAD_DIM, HEAD_DIM)
    queries = rotate(projected[:, 0].reshape(shape_heads), cosine_table, sine_timestep, 1.0).astype(
        jnp.bfloat16
    )
    key_block = rotate(
        projected[:, 1].reshape(shape_heads), cosine_table, sine_timestep, 1.0
    ).astype(jnp.bfloat16)
    value_block = projected[:, 2].reshape(shape_heads).astype(jnp.bfloat16)
    mixed_heads, log_total = attend(queries, key_block, value_block, seg_query, lengths)
    attended = mixed_heads.reshape(row_count, -1).astype(jnp.bfloat16)
    branch = reduce_heads(jnp.dot(attended, w_project_out, preferred_element_type=jnp.float32))
    resid_mid = residual_input + modulators[2] * branch
    normed_f, inv_std_f = normalize(resid_mid)
    wide_f = widen((normed_f * (1.0 + modulators[4]) + modulators[3]).astype(jnp.bfloat16))
    up_proj = jnp.dot(wide_f, w_expand, preferred_element_type=jnp.float32)
    hidden = jax.nn.gelu(up_proj, approximate=True).astype(jnp.bfloat16)
    ffn_out = reduce_heads(jnp.dot(hidden, w_reduce, preferred_element_type=jnp.float32))
    layer_out = resid_mid + modulators[5] * ffn_out
    return (
        layer_out,
        modulators,
        normed_a,
        inv_std_a,
        wide_a,
        queries,
        key_block,
        value_block,
        mixed_heads,
        log_total,
        attended,
        branch,
        normed_f,
        inv_std_f,
        wide_f,
        up_proj,
        hidden,
        ffn_out,
    )


def gelu_piece(up_proj):
    return jax.nn.gelu(up_proj, approximate=True)


def layer_backward(
    residual_input,
    modulation_vector,
    one_hot_mask,
    cosine_table,
    sine_timestep,
    seg_query,
    lengths,
    weights,
    incoming,
):
    (
        layer_out,
        modulators,
        normed_a,
        inv_std_a,
        wide_a,
        queries,
        key_block,
        value_block,
        mixed_heads,
        log_total,
        attended,
        branch,
        normed_f,
        inv_std_f,
        wide_f,
        up_proj,
        hidden,
        ffn_out,
    ) = layer_forward(
        residual_input,
        modulation_vector,
        one_hot_mask,
        cosine_table,
        sine_timestep,
        seg_query,
        lengths,
        weights,
    )
    w_proj, w_project_out, w_expand, w_reduce = weights
    row_count = residual_input.shape[0]
    d_gate_f = exact("tu,td->ud", one_hot_mask, incoming * ffn_out)
    d_ffn = widen_grad((incoming * modulators[5]).astype(jnp.bfloat16))
    g_reduce = jnp.einsum("tf,td->fd", hidden, d_ffn, preferred_element_type=jnp.float32)
    d_hidden = jnp.einsum("td,fd->tf", d_ffn, w_reduce, preferred_element_type=jnp.float32)
    gelu_value, gelu_pull = jax.vjp(gelu_piece, up_proj)
    d_up = gelu_pull(d_hidden)[0].astype(jnp.bfloat16)
    g_expand = jnp.einsum("td,tf->df", wide_f, d_up, preferred_element_type=jnp.float32)
    d_wide_f = sum_back(jnp.einsum("tf,df->td", d_up, w_expand, preferred_element_type=jnp.float32))
    d_scale_f = exact("tu,td->ud", one_hot_mask, d_wide_f * normed_f)
    d_shift_f = exact("tu,td->ud", one_hot_mask, d_wide_f)
    d_mid = incoming + norm_back(d_wide_f * (1.0 + modulators[4]), normed_f, inv_std_f)
    d_gate_a = exact("tu,td->ud", one_hot_mask, d_mid * branch)
    d_branch = widen_grad((d_mid * modulators[2]).astype(jnp.bfloat16))
    g_project_out = jnp.einsum("te,td->ed", attended, d_branch, preferred_element_type=jnp.float32)
    d_attended = jnp.einsum(
        "td,ed->te", d_branch, w_project_out, preferred_element_type=jnp.float32
    ).astype(jnp.bfloat16)
    grad_att = d_attended.reshape(queries.shape)
    row_delta = jnp.einsum("qhd,qhd->hq", grad_att.astype(jnp.float32), mixed_heads)
    grad_query, grad_key, grad_value = block_back(
        queries,
        grad_att,
        log_total,
        row_delta,
        seg_query,
        lengths,
        lax.all_gather(key_block, "seq", axis=0, tiled=True),
        lax.all_gather(value_block, "seq", axis=0, tiled=True),
    )
    piece_rows = grad_key.shape[0]
    both_grads = jnp.stack(
        [grad_key.reshape(piece_rows, -1), grad_value.reshape(piece_rows, -1)], axis=1
    )
    grad_query, buffer_all = (grad_query, both_grads)
    own_grads = lax.psum_scatter(
        buffer_all.astype(jnp.bfloat16), "seq", scatter_dimension=0, tiled=True
    ).astype(jnp.float32)
    grad_key = own_grads[:, 0].reshape(queries.shape)
    grad_value = own_grads[:, 1]
    d_proj = jnp.stack(
        [
            rotate(grad_query, cosine_table, sine_timestep, -1.0).reshape(row_count, -1),
            rotate(grad_key, cosine_table, sine_timestep, -1.0).reshape(row_count, -1),
            grad_value,
        ],
        axis=1,
    ).astype(jnp.bfloat16)
    g_proj = jnp.einsum("td,tce->dce", wide_a, d_proj, preferred_element_type=jnp.float32)
    d_wide_a = sum_back(
        jnp.einsum("tce,dce->td", d_proj, w_proj, preferred_element_type=jnp.float32)
    )
    d_scale_a = exact("tu,td->ud", one_hot_mask, d_wide_a * normed_a)
    d_shift_a = exact("tu,td->ud", one_hot_mask, d_wide_a)
    d_input = d_mid + norm_back(d_wide_a * (1.0 + modulators[1]), normed_a, inv_std_a)
    d_modul = jnp.stack([d_shift_a, d_scale_a, d_gate_a, d_shift_f, d_scale_f, d_gate_f], axis=1)
    return (d_input, (g_proj, g_project_out, g_expand, g_reduce), d_modul)


def put_slot(store, slot_index, value_new, is_valid):
    current = lax.dynamic_index_in_dim(store, slot_index, 0, keepdims=False)
    return lax.dynamic_update_index_in_dim(
        store, jnp.where(is_valid, value_new, current), slot_index, 0
    )


def local(
    frames,
    cotangent,
    utt_lengths,
    time_ids,
    w_time_in,
    w_time_out,
    w_mod,
    w_qkv,
    w_out,
    w_up,
    w_down,
):
    micro_count, row_count, narrow = frames.shape
    section_index = lax.axis_index("section")
    first_row = lax.axis_index("seq") * row_count
    weights = (w_qkv[0], w_out[0], w_up[0], w_down[0])
    mod_weight = w_mod[0].astype(jnp.float32)
    time_in = w_time_in.astype(jnp.float32)
    time_out = w_time_out.astype(jnp.float32)

    def time_activation(first_weight, second_weight):
        inner = exact("muf,fd->mud", sinusoid(time_ids), first_weight)
        return jax.nn.silu(exact("mud,de->mue", jax.nn.silu(inner), second_weight))

    temb_act = time_activation(time_in, time_out)
    modul_all = exact("mud,dce->muce", temb_act, mod_weight)

    def layout(slot_index):
        lengths = lax.dynamic_index_in_dim(utt_lengths, slot_index, 0, keepdims=False)
        segment, position, one_hot_mask = frame_layout(lengths, first_row, row_count)
        cosine_table, sine_timestep = rotation(position)
        modulation_vector = lax.dynamic_index_in_dim(modul_all, slot_index, 0, keepdims=False)
        return (lengths, segment, one_hot_mask, cosine_table, sine_timestep, modulation_vector)

    def forward_tick(carried, tick_index):
        arrived, stored, shown = carried
        slot_raw = tick_index - section_index
        is_valid = (slot_raw >= 0) & (slot_raw < micro_count)
        slot_index = jnp.clip(slot_raw, 0, micro_count - 1)
        fresh_in = lax.dynamic_index_in_dim(
            frames, jnp.minimum(tick_index, micro_count - 1), 0, keepdims=False
        )
        residual_input = jnp.where(section_index == 0, fresh_in, arrived).astype(jnp.float32)
        lengths, segment, one_hot_mask, cosine_table, sine_timestep, modulation_vector = layout(
            slot_index
        )
        result = layer_forward(
            residual_input,
            modulation_vector,
            one_hot_mask,
            cosine_table,
            sine_timestep,
            segment,
            lengths,
            weights,
        )[0].astype(jnp.bfloat16)
        stored = put_slot(stored, slot_index, residual_input, is_valid)
        shown = put_slot(shown, slot_index, result, is_valid)
        arrived = passed_along(result, "section", 1)
        return ((arrived, stored, shown), None)

    start_fwd = (
        jnp.zeros((row_count, narrow), jnp.bfloat16),
        jnp.zeros((micro_count, row_count, narrow), jnp.float32),
        jnp.zeros((micro_count, row_count, narrow), jnp.bfloat16),
    )
    (unused_arrived, stored, shown), unused_out = lax.scan(
        forward_tick, start_fwd, jnp.arange(micro_count + 1)
    )

    def backward_tick(carried, tick_index):
        arrived, slopes, grad_sums, modul_grads = carried
        slot_raw = tick_index - 1 + section_index
        is_valid = (slot_raw >= 0) & (slot_raw < micro_count)
        slot_index = jnp.clip(slot_raw, 0, micro_count - 1)
        given = lax.dynamic_index_in_dim(
            cotangent, jnp.minimum(tick_index, micro_count - 1), 0, keepdims=False
        )
        incoming = jnp.where(section_index == 1, given, arrived).astype(jnp.float32)
        lengths, segment, one_hot_mask, cosine_table, sine_timestep, modulation_vector = layout(
            slot_index
        )
        residual_input = lax.dynamic_index_in_dim(stored, slot_index, 0, keepdims=False)
        d_input, parts, d_modul = layer_backward(
            residual_input,
            modulation_vector,
            one_hot_mask,
            cosine_table,
            sine_timestep,
            segment,
            lengths,
            weights,
            incoming,
        )
        keep_scale = is_valid.astype(jnp.float32)
        grad_sums = tuple(
            (total_now + keep_scale * part for total_now, part in zip(grad_sums, parts))
        )
        modul_grads = put_slot(modul_grads, slot_index, d_modul, is_valid)
        slopes = put_slot(slopes, slot_index, d_input, is_valid)
        arrived = passed_along(d_input.astype(jnp.bfloat16), "section", -1)
        return ((arrived, slopes, grad_sums, modul_grads), None)

    zero_grads = tuple((jnp.zeros(weight.shape, jnp.float32) for weight in weights))
    start_bwd = (
        jnp.zeros((row_count, narrow), jnp.bfloat16),
        jnp.zeros((micro_count, row_count, narrow), jnp.float32),
        zero_grads,
        jnp.zeros(modul_all.shape, jnp.float32),
    )
    (unused_arrived, slopes, grad_sums, modul_grads), unused_out = lax.scan(
        backward_tick, start_bwd, jnp.arange(micro_count + 1)
    )
    g_mod_local = exact("mud,muce->dce", temb_act, modul_grads)
    partial_act = exact("muce,dce->mud", modul_grads, mod_weight)
    g_proj, g_project_out, g_expand, g_reduce, g_mod_sum = (
        lax.psum(grad_sums[0].astype(jnp.bfloat16), "seq").astype(jnp.float32),
        lax.psum(grad_sums[1].astype(jnp.bfloat16), "seq").astype(jnp.float32),
        lax.psum(grad_sums[2].astype(jnp.bfloat16), "seq").astype(jnp.float32),
        lax.psum(grad_sums[3].astype(jnp.bfloat16), "seq").astype(jnp.float32),
        lax.psum(g_mod_local.astype(jnp.bfloat16), "seq").astype(jnp.float32),
    )
    d_temb_act = lax.psum(partial_act, ("section", "seq", "heads"))
    unused_value, time_pull = jax.vjp(time_activation, time_in, time_out)
    g_first, g_second = time_pull(d_temb_act)
    return (
        shown[None],
        slopes[None],
        g_first,
        g_second,
        g_mod_sum[None],
        g_proj[None],
        g_project_out[None],
        g_expand[None],
        g_reduce[None],
    )


def solution(mesh):
    placed = (
        P(None, "seq", "heads"),
        P(None, "seq", "heads"),
        P(),
        P(),
        P(),
        P(),
        P("section", None, None, "heads"),
        P("section", None, None, "heads"),
        P("section", "heads", None),
        P("section", None, "heads"),
        P("section", "heads", None),
    )
    return jax.shard_map(
        local,
        mesh=mesh,
        in_specs=placed,
        out_specs=(
            P("section", None, "seq", "heads"),
            P("section", None, "seq", "heads"),
            P(),
            P(),
            P("section", None, None, "heads"),
            P("section", None, None, "heads"),
            P("section", "heads", None),
            P("section", None, "heads"),
            P("section", "heads", None),
        ),
        check_vma=False,
    )
```

profile of v0, /device:TPU:0, one launch (start us, length us, event | category | flops | bytes accessed | tf_op | source)
XLA Modules:
  0.0 1625.9 jit_solution(6797761314295767531)
XLA Ops:
  17.6 492.9 %while.40 = (s32[]{:T(128)}, bf16[176,256]{1,0:T(8,128)(2,1)}, f32[2,176,256]{2,1,0:T(8,128)S(1)}, bf16[2,176,256]{2,1,0:T(8,128)(2,1)}, pred[]{:T(512)}, /*inde...) while((s32[]{:T(128)}, bf16[176,256]{1,0:T(8,128)(2,1)}, ...), condition=%wide.region_13.14_spmd, body=%wide.region_0.13_spmd.sunk | while | flops 884814976 | bytes 29142512 | solution.py:403
  111.3 17.7 %reduce-scatter.8.cloned.1.call-done = bf16[176,256]{1,0:T(8,128)(2,1)} async-done(((bf16[176,1024]{1,0:T(8,128)(2,1)}), bf16[176,256]{1,0:T(8,128)(2,1)}) %reduce-scatter.8.cloned.1.call-update) | async-done | bytes 90128 | tf_op jit(solution)/shard_map/while/body/eval_jaxpr/reduce_scatter | solution.py:98
  160.7 18.7 %reduce-scatter.10.cloned.1.call-done = bf16[176,256]{1,0:T(8,128)(2,1)} async-done(((bf16[176,1024]{1,0:T(8,128)(2,1)}), bf16[176,256]{1,0:T(8,128)(2,1)}) %reduce-scatter.10.cloned.1.call-update) | async-done | bytes 90128 | tf_op jit(solution)/shard_map/while/body/eval_jaxpr/reduce_scatter | solution.py:98
  206.2 14.9 all_gather.70
  274.0 18.5 %reduce-scatter.8.cloned.1.call-done = bf16[176,256]{1,0:T(8,128)(2,1)} async-done(((bf16[176,1024]{1,0:T(8,128)(2,1)}), bf16[176,256]{1,0:T(8,128)(2,1)}) %reduce-scatter.8.cloned.1.call-update) | async-done | bytes 90128 | tf_op jit(solution)/shard_map/while/body/eval_jaxpr/reduce_scatter | solution.py:98
  304.7 14.9 all_gather.73
  324.2 18.3 %reduce-scatter.10.cloned.1.call-done = bf16[176,256]{1,0:T(8,128)(2,1)} async-done(((bf16[176,1024]{1,0:T(8,128)(2,1)}), bf16[176,256]{1,0:T(8,128)(2,1)}) %reduce-scatter.10.cloned.1.call-update) | async-done | bytes 90128 | tf_op jit(solution)/shard_map/while/body/eval_jaxpr/reduce_scatter | solution.py:98
  369.4 15.0 all_gather.70
  437.0 18.6 %reduce-scatter.8.cloned.1.call-done = bf16[176,256]{1,0:T(8,128)(2,1)} async-done(((bf16[176,1024]{1,0:T(8,128)(2,1)}), bf16[176,256]{1,0:T(8,128)(2,1)}) %reduce-scatter.8.cloned.1.call-update) | async-done | bytes 90128 | tf_op jit(solution)/shard_map/while/body/eval_jaxpr/reduce_scatter | solution.py:98
  467.9 14.9 all_gather.73
  487.4 18.5 %reduce-scatter.10.cloned.1.call-done = bf16[176,256]{1,0:T(8,128)(2,1)} async-done(((bf16[176,1024]{1,0:T(8,128)(2,1)}), bf16[176,256]{1,0:T(8,128)(2,1)}) %reduce-scatter.10.cloned.1.call-update) | async-done | bytes 90128 | tf_op jit(solution)/shard_map/while/body/eval_jaxpr/reduce_scatter | solution.py:98
  513.0 923.6 %while.41 = (s32[]{:T(128)}, bf16[176,256]{1,0:T(8,128)(2,1)}, f32[2,176,256]{2,1,0:T(8,128)}, f32[1024,3,256]{2,0,1:T(8,128)}, f32[256,1024]{1,0:T(8,128)}, /*i...) while((s32[]{:T(128)}, bf16[176,256]{1,0:T(8,128)(2,1)}, ...), condition=%wide.region_38.39_spmd.clone, body=%wide.region_14.38_spmd.clone.sunk | while | flops 2641141248 | bytes 124777184 | solution.py:447
  532.6 15.0 all_gather.74
  613.5 15.7 all_gather.77
  668.1 17.3 %reduce-scatter.14.cloned.1.call-done = bf16[176,256]{1,0:T(8,128)(2,1)} async-done(((bf16[176,1024]{1,0:T(8,128)(2,1)}), bf16[176,256]{1,0:T(8,128)(2,1)}) %reduce-scatter.14.cloned.1.call-update) | async-done | bytes 90128 | tf_op jit(solution)/shard_map/while/body/eval_jaxpr/reduce_scatter | solution.py:108
  737.0 19.3 %reduce-scatter.16.cloned.1.call-done = bf16[176,2,256]{2,0,1:T(8,128)(2,1)} async-done(((bf16[704,2,256]{2,0,1:T(8,128)(2,1)}), bf16[176,2,256]{2,0,1:T(8,128)(2,1)}) %reduce-scatter.16.cloned.1.call-update) | async-done | bytes 180240 | tf_op jit(solution)/shard_map/while/body/eval_jaxpr/reduce_scatter | solution.py:305
  921.0 15.8 all_gather.77
  975.4 17.5 %reduce-scatter.14.cloned.1.call-done = bf16[176,256]{1,0:T(8,128)(2,1)} async-done(((bf16[176,1024]{1,0:T(8,128)(2,1)}), bf16[176,256]{1,0:T(8,128)(2,1)}) %reduce-scatter.14.cloned.1.call-update) | async-done | bytes 90128 | tf_op jit(solution)/shard_map/while/body/eval_jaxpr/reduce_scatter | solution.py:108
  1044.6 19.2 %reduce-scatter.16.cloned.1.call-done = bf16[176,2,256]{2,0,1:T(8,128)(2,1)} async-done(((bf16[704,2,256]{2,0,1:T(8,128)(2,1)}), bf16[176,2,256]{2,0,1:T(8,128)(2,1)}) %reduce-scatter.16.cloned.1.call-update) | async-done | bytes 180240 | tf_op jit(solution)/shard_map/while/body/eval_jaxpr/reduce_scatter | solution.py:305
  1228.4 16.0 all_gather.77
  1283.4 17.3 %reduce-scatter.14.cloned.1.call-done = bf16[176,256]{1,0:T(8,128)(2,1)} async-done(((bf16[176,1024]{1,0:T(8,128)(2,1)}), bf16[176,256]{1,0:T(8,128)(2,1)}) %reduce-scatter.14.cloned.1.call-update) | async-done | bytes 90128 | tf_op jit(solution)/shard_map/while/body/eval_jaxpr/reduce_scatter | solution.py:108
  1352.3 19.3 %reduce-scatter.16.cloned.1.call-done = bf16[176,2,256]{2,0,1:T(8,128)(2,1)} async-done(((bf16[704,2,256]{2,0,1:T(8,128)(2,1)}), bf16[176,2,256]{2,0,1:T(8,128)(2,1)}) %reduce-scatter.16.cloned.1.call-update) | async-done | bytes 180240 | tf_op jit(solution)/shard_map/while/body/eval_jaxpr/reduce_scatter | solution.py:305
  1452.5 39.1 %psum.154 = f32[2,3,1024]{2,1,0:T(4,128)S(1)} all-reduce(f32[2,3,1024]{2,1,0:T(4,128)S(1)} %fusion.158), channel_id=1, replica_groups=mesh['section'=2,'seq'=4,'heads'=4] {'section','seq','heads'}, use_global_device_ids=true, to_apply=%region_39.40 | all-reduce | flops 6144 | bytes 49152 | tf_op jit(solution)/shard_map/psum | solution.py:459
  1502.1 104.4 %all-reduce.21.cloned.1.call-done = (bf16[1,1024,6,256]{3,1,2,0:T(8,128)(2,1)}, bf16[1,1024,3,256]{3,1,2,0:T(8,128)(2,1)}, bf16[1,256,1024]{2,1,0:T(8,128)(2,1)}...) async-done(((bf16[1,1024,6,256]{3,1,2,0:T(8,128)(2,1)}, bf16[1,1024,3,256]{3,1,2,0:T(8,128)(2,1)}, bf16[1,256,1024]{2,1,0:T(8,128)(2,1)}, ...) | async-done | bytes 7340048 | tf_op jit(solution)/shard_map/psum | solution.py:457
  (790 shorter events, 1106.6 us)
Async XLA Ops:
  17.6 111.4 %reduce-scatter.8.cloned.1.call-start = ((), (), s32[]{:S(2)}) async-start(), calls=%async_computation.8 | async-start | bytes 450560 | tf_op jit(solution)/shard_map/while/body/eval_jaxpr/reduce_scatter | solution.py:98
  111.2 68.2 %reduce-scatter.10.cloned.1.call-start = ((), (), s32[]{:S(2)}) async-start(), calls=%async_computation.9 | async-start | bytes 450560 | tf_op jit(solution)/shard_map/while/body/eval_jaxpr/reduce_scatter | solution.py:98
  183.9 108.5 %reduce-scatter.8.cloned.1.call-start = ((), (), s32[]{:S(2)}) async-start(), calls=%async_computation.8 | async-start | bytes 450560 | tf_op jit(solution)/shard_map/while/body/eval_jaxpr/reduce_scatter | solution.py:98
  274.0 68.6 %reduce-scatter.10.cloned.1.call-start = ((), (), s32[]{:S(2)}) async-start(), calls=%async_computation.9 | async-start | bytes 450560 | tf_op jit(solution)/shard_map/while/body/eval_jaxpr/reduce_scatter | solution.py:98
  347.1 108.6 %reduce-scatter.8.cloned.1.call-start = ((), (), s32[]{:S(2)}) async-start(), calls=%async_computation.8 | async-start | bytes 450560 | tf_op jit(solution)/shard_map/while/body/eval_jaxpr/reduce_scatter | solution.py:98
  437.0 69.0 %reduce-scatter.10.cloned.1.call-start = ((), (), s32[]{:S(2)}) async-start(), calls=%async_computation.9 | async-start | bytes 450560 | tf_op jit(solution)/shard_map/while/body/eval_jaxpr/reduce_scatter | solution.py:98
  513.4 119.3 %reduce-scatter.12.cloned.1.call-start = ((), (), s32[]{:S(2)}) async-start(), calls=%async_computation.10 | async-start | bytes 450560 | tf_op jit(solution)/shard_map/while/body/eval_jaxpr/reduce_scatter | solution.py:98
  610.3 75.0 %reduce-scatter.14.cloned.1.call-start = ((), (), s32[]{:S(2)}) async-start(), calls=%async_computation.11 | async-start | bytes 450560 | tf_op jit(solution)/shard_map/while/body/eval_jaxpr/reduce_scatter | solution.py:108
  666.7 89.5 %reduce-scatter.16.cloned.1.call-start = ((), (), s32[]{:S(2)}) async-start(), calls=%async_computation.12 | async-start | bytes 901120 | tf_op jit(solution)/shard_map/while/body/eval_jaxpr/reduce_scatter | solution.py:305
  731.0 66.1 %reduce-scatter.18.cloned.1.call-start = ((), (), s32[]{:S(2)}) async-start(), calls=%async_computation.13 | async-start | bytes 450560 | tf_op jit(solution)/shard_map/while/body/eval_jaxpr/reduce_scatter | solution.py:108
  776.6 42.1 %reduce-scatter.20.cloned.1.call-start = ((), (), s32[]{:S(2)}) async-start(), calls=%async_computation.14 | async-start | bytes 450560 | tf_op jit(solution)/shard_map/while/body/eval_jaxpr/reduce_scatter | solution.py:98
  809.1 12.2 collective-permute-start.1
  821.3 118.9 %reduce-scatter.12.cloned.1.call-start = ((), (), s32[]{:S(2)}) async-start(), calls=%async_computation.10 | async-start | bytes 450560 | tf_op jit(solution)/shard_map/while/body/eval_jaxpr/reduce_scatter | solution.py:98
  917.8 75.2 %reduce-scatter.14.cloned.1.call-start = ((), (), s32[]{:S(2)}) async-start(), calls=%async_computation.11 | async-start | bytes 450560 | tf_op jit(solution)/shard_map/while/body/eval_jaxpr/reduce_scatter | solution.py:108
  974.1 89.7 %reduce-scatter.16.cloned.1.call-start = ((), (), s32[]{:S(2)}) async-start(), calls=%async_computation.12 | async-start | bytes 901120 | tf_op jit(solution)/shard_map/while/body/eval_jaxpr/reduce_scatter | solution.py:305
  1038.6 66.0 %reduce-scatter.18.cloned.1.call-start = ((), (), s32[]{:S(2)}) async-start(), calls=%async_computation.13 | async-start | bytes 450560 | tf_op jit(solution)/shard_map/while/body/eval_jaxpr/reduce_scatter | solution.py:108
  1084.1 41.9 %reduce-scatter.20.cloned.1.call-start = ((), (), s32[]{:S(2)}) async-start(), calls=%async_computation.14 | async-start | bytes 450560 | tf_op jit(solution)/shard_map/while/body/eval_jaxpr/reduce_scatter | solution.py:98
  1128.6 119.2 %reduce-scatter.12.cloned.1.call-start = ((), (), s32[]{:S(2)}) async-start(), calls=%async_computation.10 | async-start | bytes 450560 | tf_op jit(solution)/shard_map/while/body/eval_jaxpr/reduce_scatter | solution.py:98
  1225.2 75.5 %reduce-scatter.14.cloned.1.call-start = ((), (), s32[]{:S(2)}) async-start(), calls=%async_computation.11 | async-start | bytes 450560 | tf_op jit(solution)/shard_map/while/body/eval_jaxpr/reduce_scatter | solution.py:108
  1282.0 89.5 %reduce-scatter.16.cloned.1.call-start = ((), (), s32[]{:S(2)}) async-start(), calls=%async_computation.12 | async-start | bytes 901120 | tf_op jit(solution)/shard_map/while/body/eval_jaxpr/reduce_scatter | solution.py:305
  1346.3 66.3 %reduce-scatter.18.cloned.1.call-start = ((), (), s32[]{:S(2)}) async-start(), calls=%async_computation.13 | async-start | bytes 450560 | tf_op jit(solution)/shard_map/while/body/eval_jaxpr/reduce_scatter | solution.py:108
  1391.9 42.0 %reduce-scatter.20.cloned.1.call-start = ((), (), s32[]{:S(2)}) async-start(), calls=%async_computation.14 | async-start | bytes 450560 | tf_op jit(solution)/shard_map/while/body/eval_jaxpr/reduce_scatter | solution.py:98
  1424.4 12.1 collective-permute-start.1
  1436.6 169.9 %all-reduce.21.cloned.1.call-start = ((), (), s32[]{:S(2)}) async-start(), calls=%async_computation.7 | async-start | bytes 14680064 | tf_op jit(solution)/shard_map/psum | solution.py:457
  (129 other events, 718.4 us)
Sparse Core Ops, SparseCore 0:
  111.3 17.6 reduce-scatter.7
  159.3 20.0 reduce-scatter.9
  274.1 18.3 reduce-scatter.7
  322.8 19.6 reduce-scatter.9
  437.1 18.5 reduce-scatter.7
  486.0 19.9 reduce-scatter.9
  610.5 19.3 reduce-scatter.11
  666.8 18.4 reduce-scatter.13
  731.1 25.1 reduce-scatter.15
  776.7 20.2 reduce-scatter.17
  800.0 18.7 reduce-scatter.19
  917.9 19.7 reduce-scatter.11
  974.2 18.6 reduce-scatter.13
  1038.7 25.0 reduce-scatter.15
  1084.2 20.2 reduce-scatter.17
  1107.4 18.5 reduce-scatter.19
  1225.3 19.8 reduce-scatter.11
  1282.1 18.4 reduce-scatter.13
  1346.4 25.1 reduce-scatter.15
  1392.0 20.5 reduce-scatter.17
  1415.5 18.3 reduce-scatter.19
Sparse Core Ops, SparseCore 1:
  1450.0 156.5 all-reduce.20
where the time goes:
time: 1650 us; the launch traced here: 1630 us
  blocking collectives  619 us (38%)
  waiting for transfers between devices  350 us (21%)
  matrix products  231 us (14%)
  local copies, waits for them, and re-layouts  227 us (14%)
  other arithmetic  156 us (9%)
  loops' own time  17.6 us (1%)
    all_gather x12, blocking collectives, widen(): return lax.all_gather(narrow_part, 'heads', axis=1, tiled=True)  175 us
    psum x18, blocking collectives, across_heads(): return lax.psum((first_sum, second_sum), 'heads')  170 us
    reduce_scatter x12, waiting for transfers between devices, reduce_heads(): lax.psum_scatter(term.astype(jnp.bfloat16), 'heads', scatter_dimension=1,...  117 us
    psum x1, waiting for transfers between devices, local(): lax.psum(g_mod_local.astype(jnp.bfloat16), 'seq').astype(jnp.float32)  104 us
    all_gather x6, blocking collectives, widen_grad(): return lax.all_gather(narrow_part, 'heads', axis=1, tiled=True)  90.1 us
    dot_general x62, matrix products, exact(): return jnp.einsum(spec, left, right, precision=lax.Precision.HIGHEST)  85.9 us
    all_gather x6, blocking collectives, attend(): lax.all_gather(key_block, 'seq', axis=0, tiled=True)  76.3 us
    all_gather x6, blocking collectives, attend(): lax.all_gather(value_block, 'seq', axis=0, tiled=True)  68.5 us
  transfers between devices with their start and end apart: 28, of which 22 were waited for; matrix products, arithmetic and copies ran while one was open for 8% of the time, Pallas kernels for 0%

commit v1 on v0

v1 whole, which is shorter than its diff:
```python
import functools
import math

import jax
import jax.numpy as jnp
import numpy as np
from jax import lax
from jax.experimental import pallas as pl
from jax.experimental.pallas import tpu as pltpu
from jax.sharding import PartitionSpec as P

HEAD_DIM = 64
FREQ = 256
EPS = 1e-06
BF = jnp.bfloat16
F32 = jnp.float32
MIB = 1024 * 1024


def shifted(value, axis, by):
    length = lax.axis_size(axis)
    if by % length == 0:
        return value
    return lax.ppermute(value, axis, [(i, (i + by) % length) for i in range(length)])


def gather(value, axis):
    return [shifted(value, axis, k) for k in range(lax.axis_size(axis))]


def exchange(chunks, axis):
    return [shifted(chunk, axis, k) for k, chunk in enumerate(chunks)]


def pair_shift(value, axis, by):
    length = lax.axis_size(axis)
    pairs = [
        (c * length + i, (1 - c) * length + (i + by) % length)
        for c in range(2)
        for i in range(length)
    ]
    return lax.ppermute(value, ("section", axis), pairs)


def pair_gather(value, axis):
    return [pair_shift(value, axis, k) for k in range(lax.axis_size(axis))]


def swap(value):
    return lax.ppermute(value, "section", [(0, 1), (1, 0)])


def owner_shift(value, layer, by):
    length = lax.axis_size("seq")
    if by % length == 0:
        return value
    base = layer * length
    pairs = [(base + i, base + (i + by) % length) for i in range(length)]
    return lax.ppermute(value, ("section", "seq"), pairs)


def add_chunks(chunks):
    total = chunks[0].astype(F32)
    for chunk in chunks[1:]:
        total = total + chunk.astype(F32)
    return total.astype(BF)


def dot(left, right, contract=((1,), (0,))):
    return lax.dot_general(left, right, (contract, ((), ())), preferred_element_type=F32)


def split3(value):
    high = value.astype(BF)
    rest = value - high.astype(F32)
    middle = rest.astype(BF)
    low = (rest - middle.astype(F32)).astype(BF)
    return high, middle, low


def exact_dot(left, right, contract=((1,), (0,))):
    rows = left.shape[0]
    stacked = jnp.concatenate(split3(left), axis=0)
    out = dot(stacked, right, contract)
    return out[:rows] + (out[rows : 2 * rows] + out[2 * rows :])


def exact_outer(left, right):
    a = split3(left)
    b = split3(right)
    order = ((0, 0), (0, 1), (1, 0), (1, 1), (0, 2), (2, 0))
    tall = jnp.concatenate([a[i] for i, _ in order], axis=0)
    wide = jnp.concatenate([b[j] for _, j in order], axis=0)
    return dot(tall, wide, ((0,), (0,)))


def segments(sc, shape, axis, first):
    index = lax.broadcasted_iota(jnp.int32, shape, axis) + first
    return (index >= sc[3]).astype(jnp.int32) + (index >= sc[4]).astype(jnp.int32)


def spread(mod, sc, layer, which, seg):
    base = sc[2] * 4
    rows = [mod[layer, which, pl.ds(base + u, 1), :] for u in range(3)]
    return jnp.where(seg == 0, rows[0], jnp.where(seg == 1, rows[1], rows[2]))


def spread_narrow(mod, sc, layer, which, seg, columns):
    block = mod[layer, which, :, columns]
    index = lax.broadcasted_iota(jnp.int32, block.shape, 0) - sc[2] * 4
    rows = [
        jnp.sum(jnp.where(index == u, block, 0.0), axis=0, keepdims=True) for u in range(3)
    ]
    return jnp.where(seg == 0, rows[0], jnp.where(seg == 1, rows[1], rows[2]))


def utterance_sums(value, seg):
    rows = [
        jnp.sum(jnp.where(seg == u, value, 0.0), axis=0, keepdims=True) for u in range(3)
    ]
    return jnp.concatenate(rows + [jnp.zeros_like(rows[0])], axis=0)


def norm_of(value):
    mean = jnp.mean(value, axis=1, keepdims=True)
    centred = value - mean
    inv = lax.rsqrt(jnp.mean(centred * centred, axis=1, keepdims=True) + EPS)
    return centred * inv, inv


def norm_pull(grad, normed, inv):
    return inv * (
        grad
        - jnp.mean(grad, axis=1, keepdims=True)
        - normed * jnp.mean(grad * normed, axis=1, keepdims=True)
    )


def lanes_of(index, count, width):
    return pl.ds(pl.multiple_of(lax.rem(index, count) * width, width), width)


def place(buffer, chunks, own, width):
    count = len(chunks)
    for k, chunk in enumerate(chunks):
        buffer[:, lanes_of(own - k + count, count, width)] = chunk[...].astype(buffer.dtype)


def hand_out(outs, buffer, own, width):
    count = len(outs)
    for k, out in enumerate(outs):
        out[...] = buffer[:, lanes_of(own + k, count, width)].astype(out.dtype)


class Fetch:
    def __init__(self, sc, layer, own, other, buffer, sem):
        self.copy = pltpu.make_async_copy(own, buffer, sem)
        other_copy = pltpu.make_async_copy(other, buffer, sem)

        @pl.when(sc[2] == layer)
        def _():
            self.copy.start()

        @pl.when(sc[2] != layer)
        def _():
            other_copy.start()

    def wait(self):
        self.copy.wait()


def turn(value, cosine, sine):
    width = value.shape[1]
    even = lax.broadcasted_iota(jnp.int32, value.shape, 1) % 2 == 0
    swapped = jnp.where(even, pltpu.roll(value, width - 1, 1), pltpu.roll(value, 1, 1))
    return value * cosine + swapped * sine


def widen_table(table, width):
    copies = width // table.shape[1]
    return jnp.concatenate([table] * copies, axis=1) if copies > 1 else table[:, :width]


VM = pl.BlockSpec(memory_space=pltpu.VMEM)
SM = pl.BlockSpec(memory_space=pltpu.SMEM)
HB = pl.BlockSpec(memory_space=pl.ANY)


def sds(shape, dtype):
    return jax.ShapeDtypeStruct(tuple(shape), dtype)


def call(body, ins, specs, outs, scratch=(), flops=0, limit=24, name=None):
    moved = sum(math.prod(a.shape) * a.dtype.itemsize for a in list(ins) + list(outs))
    return pl.pallas_call(
        body,
        out_shape=list(outs),
        in_specs=list(specs),
        out_specs=[VM] * len(outs),
        scratch_shapes=list(scratch),
        compiler_params=pltpu.CompilerParams(vmem_limit_bytes=limit * MIB),
        cost_estimate=pl.CostEstimate(
            flops=int(flops), bytes_accessed=int(moved), transcendentals=0
        ),
        name=name,
    )(*ins)


def cut(refs, *counts):
    out = []
    at = 0
    for n in counts:
        if n == 1:
            out.append(refs[at])
        else:
            out.append(refs[at : at + n])
        at += n
    assert at == len(refs)
    return out


class Group(list):
    pass


def time_forward(sinus, time_in, time_out, mod_weight):
    rows, width = sinus.shape[0], time_in.shape[1]
    kinds, _, narrow = mod_weight.shape

    def body(sinus, time_in, time_out, mod_weight, inner_out, outer_out, act_out, modul):
        inner = exact_dot(sinus[...], time_in[...])
        inner_out[...] = inner
        hidden = inner / (1.0 + jnp.exp(-inner))
        outer = exact_dot(hidden, time_out[...])
        outer_out[...] = outer
        act = outer / (1.0 + jnp.exp(-outer))
        act_out[...] = act
        for which in range(kinds):
            modul[which] = exact_dot(act, mod_weight[which])

    return call(
        body,
        [sinus, time_in, time_out, mod_weight],
        [VM] * 4,
        [sds((rows, width), F32)] * 3 + [sds((kinds, rows, narrow), F32)],
        flops=2 * 256 * 4_000_000,
        name="time_forward",
    )


def collect_modulation(sc, own, other):
    count = len(own)
    kinds, rows, narrow = own[0].shape

    def body(sc, *refs):
        own, other, out = refs[:count], refs[count : 2 * count], refs[2 * count]
        for k in range(count):
            columns = lanes_of(sc[0] - k + count, count, narrow)
            for layer in range(2):
                out[layer, :, :, columns] = jnp.where(
                    sc[2] == layer, own[k][...], other[k][...]
                )

    return call(
        body,
        [sc] + own + other,
        [SM] + [VM] * (2 * count),
        [sds((2, kinds, rows, narrow * count), F32)],
        name="collect_modulation",
    )[0]


def project(dims, layer, sc, pieces, mod, w_own, w_other, cosine, sine):
    first = layer == 0
    rows, width, narrow, local = dims.rows, dims.width, dims.narrow, dims.local
    count, n_seq, n_out = dims.n_heads, dims.n_seq, dims.n_chunks
    n_in = len(pieces)

    def body(sc, *refs):
        pieces = refs[:n_in]
        mod, w_own, w_other, cosine, sine = refs[n_in : n_in + 5]
        outs = refs[n_in + 5 :]
        x_out, narrow_out, xa_out = outs[:3]
        chunks = outs[3 : 3 + n_out]
        buffer, weight, ready, sem = outs[3 + n_out :]
        fetch = Fetch(sc, layer, w_own, w_other, weight, sem)
        own_row = sc[1] * rows
        seg = segments(sc, (rows, 1), 0, own_row)
        if first:
            place(buffer, pieces, sc[0], narrow)
            x = buffer[...]
            x_out[...] = x.astype(BF)
            narrow_out[...] = pieces[0][...]
        else:
            place(buffer, pieces[1:], sc[0], narrow)
            x = pieces[0][...] + spread(mod, sc, 0, 5, seg) * buffer[...]
            low = x.astype(BF)
            x_out[...] = low
            x = low.astype(F32)
            buffer[...] = x
            narrow_out[...] = buffer[:, lanes_of(sc[0], count, narrow)].astype(BF)
        normed, _ = norm_of(x)
        xa = (normed * (1.0 + spread(mod, sc, layer, 1, seg)) + spread(mod, sc, layer, 0, seg)).astype(BF)
        xa_out[...] = xa
        here = pl.ds(pl.multiple_of(own_row, 8), rows)
        cos = widen_table(cosine[here, :], local)
        sin = widen_table(sine[here, :], local)
        fetch.wait()
        q = turn(dot(xa, weight[0]), cos, sin).astype(BF)
        k = turn(dot(xa, weight[1]), cos, sin).astype(BF)
        v = dot(xa, weight[2]).astype(BF)
        if dims.spread_heads:
            wide = local // n_seq
            for j in range(n_seq):
                part = slice(j * wide, (j + 1) * wide)
                ready[j] = jnp.concatenate([q[:, part], k[:, part], v[:, part]], axis=1)
            for j in range(n_seq):
                chunks[j][...] = ready[lax.rem(sc[1] + j, n_seq)]
        else:
            chunks[0][...] = q
            chunks[1][...] = jnp.concatenate([k, v], axis=1)

    if dims.spread_heads:
        outs = [sds((rows, 3 * local // n_seq), BF)] * n_seq
        ready = pltpu.VMEM((n_seq, rows, 3 * local // n_seq), BF)
    else:
        outs = [sds((rows, local), BF), sds((rows, 2 * local), BF)]
        ready = pltpu.VMEM((8, 128), BF)
    return call(
        body,
        [sc] + pieces + [mod, w_own, w_other, cosine, sine],
        [SM] + [VM] * n_in + [VM, HB, HB, VM, VM],
        [sds((rows, width), BF), sds((rows, narrow), BF), sds((rows, width), BF)] + outs,
        [
            pltpu.VMEM((rows, width), F32),
            pltpu.VMEM(w_own.shape, BF),
            ready,
            pltpu.SemaphoreType.DMA,
        ],
        flops=6 * rows * width * local,
        name=f"project_{layer}",
    )


def attend(dims, sc, chunks, queries):
    rows, n_seq, frames = dims.rows, dims.n_seq, dims.frames
    heads = dims.heads_here
    wide = heads * HEAD_DIM
    shared = dims.spread_heads
    blocks = n_seq if shared else 1
    n_chunks = len(chunks)
    parts = 3 if shared else 2

    def body(sc, *refs):
        chunks = refs[:n_chunks]
        rest = refs[n_chunks:]
        if not shared:
            queries, rest = rest[0], rest[1:]
        kept, probs = rest[:2]
        outs = rest[2 : 2 + blocks]
        (mixed,) = rest[2 + blocks :]
        for k in range(n_chunks):
            at = pl.multiple_of(lax.rem(sc[1] - k + n_seq, n_seq) * rows, rows)
            kept[pl.ds(at, rows), :] = chunks[k][...]
        key_seg = segments(sc, (1, frames), 1, 0)
        for block in range(blocks):
            if shared:
                here = slice(block * rows, (block + 1) * rows)
                seg = segments(sc, (rows, 1), 0, block * rows)
            else:
                here = slice(0, rows)
                seg = segments(sc, (rows, 1), 0, sc[1] * rows)
            same = seg == key_seg
            for head in range(heads):
                cols = slice(head * HEAD_DIM, (head + 1) * HEAD_DIM)
                base = (parts - 2) * wide
                key = kept[:, base + head * HEAD_DIM : base + (head + 1) * HEAD_DIM]
                base = (parts - 1) * wide
                val = kept[:, base + head * HEAD_DIM : base + (head + 1) * HEAD_DIM]
                q = kept[here, cols] if shared else queries[:, cols]
                scores = dot(q, key, ((1,), (1,))) * (1.0 / math.sqrt(HEAD_DIM))
                scores = jnp.where(same, scores, -1e30)
                weight = jnp.exp(scores - jnp.max(scores, axis=1, keepdims=True))
                weight = weight * (1.0 / jnp.sum(weight, axis=1, keepdims=True))
                low = weight.astype(BF)
                probs[head, here, :] = low
                mixed[block, :, cols] = dot(low, val).astype(BF)
        if shared:
            for k in range(n_seq):
                outs[k][...] = mixed[lax.rem(sc[1] + k, n_seq)]
        else:
            outs[0][...] = mixed[0]

    q_rows = blocks * rows
    ins = [sc] + chunks + ([] if shared else [queries])
    return call(
        body,
        ins,
        [SM] + [VM] * (len(ins) - 1),
        [sds((frames, parts * wide), BF), sds((heads, q_rows, frames), BF)]
        + [sds((rows, wide), BF)] * blocks,
        [pltpu.VMEM((blocks, rows, wide), BF)],
        flops=4 * heads * q_rows * frames * HEAD_DIM,
        name="attend",
    )


def put_heads(dims, sc, chunks, ready):
    n_seq = dims.n_seq
    if not dims.spread_heads:
        return chunks[0][...]
    for k in range(n_seq):
        ready[lax.rem(sc[1] - k + n_seq, n_seq)] = chunks[k][...]
    return jnp.concatenate([ready[j] for j in range(n_seq)], axis=1)


def project_out(dims, layer, sc, chunks, w_own, w_other):
    rows, width, narrow, local, count = (
        dims.rows, dims.width, dims.narrow, dims.local, dims.n_heads,
    )
    n_in = len(chunks)

    def body(sc, *refs):
        chunks = refs[:n_in]
        w_own, w_other, att_out = refs[n_in : n_in + 3]
        outs = refs[n_in + 3 : n_in + 3 + count]
        weight, ready, buffer, sem = refs[n_in + 3 + count :]
        fetch = Fetch(sc, layer, w_own, w_other, weight, sem)
        att = put_heads(dims, sc, chunks, ready)
        att_out[...] = att
        fetch.wait()
        buffer[...] = dot(att, weight[...]).astype(BF)
        hand_out(outs, buffer, sc[0], narrow)

    return call(
        body,
        [sc] + chunks + [w_own, w_other],
        [SM] + [VM] * n_in + [HB, HB],
        [sds((rows, local), BF)] + [sds((rows, narrow), BF)] * count,
        [
            pltpu.VMEM(w_own.shape, BF),
            pltpu.VMEM((n_in,) + chunks[0].shape, BF),
            pltpu.VMEM((rows, width), BF),
            pltpu.SemaphoreType.DMA,
        ],
        flops=2 * rows * width * local,
        name=f"project_out_{layer}",
    )


def feed_forward(dims, layer, sc, x, branch, mod, up, down):
    rows, width, narrow, count, hidden = (
        dims.rows, dims.width, dims.narrow, dims.n_heads, dims.hidden,
    )

    def body(sc, x, *refs):
        branch = refs[:count]
        mod, up_own, up_other, down_own, down_other = refs[count : count + 5]
        x1_out, xf_out, h_out, slope_out = refs[count + 5 : count + 9]
        outs = refs[count + 9 : 2 * count + 9]
        up, down, buffer, low, sem_up, sem_down = refs[2 * count + 9 :]
        fetch_up = Fetch(sc, layer, up_own, up_other, up, sem_up)
        fetch_down = Fetch(sc, layer, down_own, down_other, down, sem_down)
        seg = segments(sc, (rows, 1), 0, sc[1] * rows)
        place(buffer, branch, sc[0], narrow)
        x1 = x[...].astype(F32) + spread(mod, sc, layer, 2, seg) * buffer[...]
        x1_out[...] = x1
        normed, _ = norm_of(x1)
        xf = (normed * (1.0 + spread(mod, sc, layer, 4, seg)) + spread(mod, sc, layer, 3, seg)).astype(BF)
        xf_out[...] = xf
        fetch_up.wait()
        a = dot(xf, up[...])
        c0 = math.sqrt(2.0 / math.pi)
        square = a * a
        t = jnp.tanh(c0 * (a + 0.044715 * (a * square)))
        h = (0.5 * a * (1.0 + t)).astype(BF)
        h_out[...] = h
        slope_out[...] = 0.5 * (1.0 + t) + 0.5 * a * (1.0 - t * t) * (
            c0 * (1.0 + 3.0 * 0.044715 * square)
        )
        fetch_down.wait()
        low[...] = dot(h, down[...]).astype(BF)
        hand_out(outs, low, sc[0], narrow)

    return call(
        body,
        [sc, x] + branch + [mod, up[0], up[1], down[0], down[1]],
        [SM, VM] + [VM] * count + [VM, HB, HB, HB, HB],
        [
            sds((rows, width), F32),
            sds((rows, width), BF),
            sds((rows, hidden), BF),
            sds((rows, hidden), F32),
        ]
        + [sds((rows, narrow), BF)] * count,
        [
            pltpu.VMEM(up[0].shape, BF),
            pltpu.VMEM(down[0].shape, BF),
            pltpu.VMEM((rows, width), F32),
            pltpu.VMEM((rows, width), BF),
            pltpu.SemaphoreType.DMA,
            pltpu.SemaphoreType.DMA,
        ],
        flops=4 * rows * width * hidden,
        name=f"feed_forward_{layer}",
    )


def feed_backward(dims, layer, sc, pieces, slope, mod, up, down):
    rows, width, narrow, count, hidden = (
        dims.rows, dims.width, dims.narrow, dims.n_heads, dims.hidden,
    )
    last = layer == 1
    n_in = len(pieces)
    n_extra = 0 if last else 2

    def body(sc, *refs):
        pieces = refs[:n_in]
        slope, mod, up_own, up_other, down_own, down_other = refs[n_in : n_in + 6]
        rest = refs[n_in + 6 :]
        g_out, dz_out, da_out = rest[:3]
        outs = rest[3 : 3 + count]
        extra = rest[3 + count : 3 + count + n_extra]
        up, down, buffer, low, other_buffer, sem_up, sem_down = rest[3 + count + n_extra :]
        fetch_down = Fetch(sc, layer, down_own, down_other, down, sem_down)
        fetch_up = Fetch(sc, layer, up_own, up_other, up, sem_up)
        seg = segments(sc, (rows, 1), 0, sc[1] * rows)
        place(buffer, pieces[:count], sc[0], narrow)
        if last:
            g = buffer[...]
            g_out[...] = g.astype(BF)
        else:
            x, d_mid = pieces[count:]
            grad_out, sums_out = extra
            dxa = buffer[...]
            normed, inv = norm_of(x[...].astype(F32))
            other_buffer[...] = dxa * normed
            mine = lanes_of(sc[0], count, narrow)
            sums_out[0] = utterance_sums(buffer[:, mine], seg)
            sums_out[1] = utterance_sums(other_buffer[:, mine], seg)
            dx = d_mid[...] + norm_pull(
                dxa * (1.0 + spread(mod, sc, 1, 1, seg)), normed, inv
            )
            other_buffer[...] = dx
            grad_out[...] = other_buffer[:, mine]
            g = dx.astype(BF)
            g_out[...] = g
            g = g.astype(F32)
        dz = (g * spread(mod, sc, layer, 5, seg)).astype(BF)
        dz_out[...] = dz
        fetch_down.wait()
        da = (dot(dz, down[...], ((1,), (1,))) * slope[...]).astype(BF)
        da_out[...] = da
        fetch_up.wait()
        low[...] = dot(da, up[...], ((1,), (1,))).astype(BF)
        hand_out(outs, low, sc[0], narrow)

    extra = [] if last else [sds((rows, narrow), F32), sds((2, 4, narrow), F32)]
    return call(
        body,
        [sc] + pieces + [slope, mod, up[0], up[1], down[0], down[1]],
        [SM] + [VM] * n_in + [VM, VM, HB, HB, HB, HB],
        [sds((rows, width), BF), sds((rows, width), BF), sds((rows, hidden), BF)]
        + [sds((rows, narrow), BF)] * count
        + extra,
        [
            pltpu.VMEM(up[0].shape, BF),
            pltpu.VMEM(down[0].shape, BF),
            pltpu.VMEM((rows, width), F32),
            pltpu.VMEM((rows, width), BF),
            pltpu.VMEM((rows, width), F32),
            pltpu.SemaphoreType.DMA,
            pltpu.SemaphoreType.DMA,
        ],
        flops=4 * rows * width * hidden,
        name=f"feed_backward_{layer}",
    )


def middle_backward(dims, layer, sc, g, x1, sums, branch, mod, w_own, w_other):
    rows, width, narrow, local, count = (
        dims.rows, dims.width, dims.narrow, dims.local, dims.n_heads,
    )
    n_seq = dims.n_seq
    n_out = n_seq if dims.spread_heads else 1

    def body(sc, g, x1, *refs):
        sums = refs[:count]
        branch, mod, w_own, w_other = refs[count : count + 4]
        d_mid_out, dy_out, small = refs[count + 4 : count + 7]
        outs = refs[count + 7 : count + 7 + n_out]
        weight, buffer, other, ready, sem = refs[count + 7 + n_out :]
        fetch = Fetch(sc, layer, w_own, w_other, weight, sem)
        seg = segments(sc, (rows, 1), 0, sc[1] * rows)
        mine = lanes_of(sc[0], count, narrow)
        place(buffer, sums, sc[0], narrow)
        dxf = buffer[...]
        normed, inv = norm_of(x1[...])
        other[...] = dxf * normed
        small[1] = utterance_sums(buffer[:, mine], seg)
        small[2] = utterance_sums(other[:, mine], seg)
        d_mid = g[...].astype(F32) + norm_pull(
            dxf * (1.0 + spread(mod, sc, layer, 4, seg)), normed, inv
        )
        d_mid_out[...] = d_mid
        other[...] = d_mid
        small[0] = utterance_sums(other[:, mine] * branch[...].astype(F32), seg)
        dy = (d_mid * spread(mod, sc, layer, 2, seg)).astype(BF)
        dy_out[...] = dy
        fetch.wait()
        datt = dot(dy, weight[...], ((1,), (1,))).astype(BF)
        if dims.spread_heads:
            wide = local // n_seq
            for j in range(n_seq):
                ready[j] = datt[:, j * wide : (j + 1) * wide]
            for k in range(n_seq):
                outs[k][...] = ready[lax.rem(sc[1] + k, n_seq)]
        else:
            outs[0][...] = datt

    wide = local // n_out
    return call(
        body,
        [sc, g, x1] + sums + [branch, mod, w_own, w_other],
        [SM, VM, VM] + [VM] * count + [VM, VM, HB, HB],
        [sds((rows, width), F32), sds((rows, width), BF), sds((3, 4, narrow), F32)]
        + [sds((rows, wide), BF)] * n_out,
        [
            pltpu.VMEM(w_own.shape, BF),
            pltpu.VMEM((rows, width), F32),
            pltpu.VMEM((rows, width), F32),
            pltpu.VMEM((n_out, rows, wide), BF),
            pltpu.SemaphoreType.DMA,
        ],
        flops=2 * rows * width * local,
        name=f"middle_backward_{layer}",
    )


def attend_backward(dims, sc, chunks, queries, kept, probs, cosine, sine):
    rows, n_seq, frames = dims.rows, dims.n_seq, dims.frames
    heads = dims.heads_here
    wide = heads * HEAD_DIM
    shared = dims.spread_heads
    n_in = len(chunks)
    q_rows = frames if shared else rows
    parts = 3 if shared else 2
    scale = 1.0 / math.sqrt(HEAD_DIM)

    def body(sc, *refs):
        chunks = refs[:n_in]
        rest = refs[n_in:]
        if not shared:
            queries, rest = rest[0], rest[1:]
        kept, probs, cosine, sine = rest[:4]
        rest = rest[4:]
        if not shared:
            q_out, rest = rest[0], rest[1:]
        outs = rest[:n_seq]
        grad, done, d_score = rest[n_seq:]
        if shared:
            for k in range(n_in):
                at = pl.multiple_of(lax.rem(sc[1] - k + n_seq, n_seq) * rows, rows)
                grad[pl.ds(at, rows), :] = chunks[k][...]
            cos = cosine[:, :HEAD_DIM]
            sin = -sine[:, :HEAD_DIM]
            cos_q, sin_q = cos, sin
        else:
            grad[...] = chunks[0][...]
            cos = cosine[:, :HEAD_DIM]
            sin = -sine[:, :HEAD_DIM]
            here = pl.ds(pl.multiple_of(sc[1] * rows, 8), rows)
            cos_q = cosine[here, :HEAD_DIM]
            sin_q = -sine[here, :HEAD_DIM]
        for head in range(heads):
            cols = slice(head * HEAD_DIM, (head + 1) * HEAD_DIM)
            base = (parts - 2) * wide + head * HEAD_DIM
            key = kept[:, base : base + HEAD_DIM]
            base = (parts - 1) * wide + head * HEAD_DIM
            val = kept[:, base : base + HEAD_DIM]
            q = kept[:, cols] if shared else queries[:, cols]
            for at in range(0, q_rows, rows):
                here = slice(at, at + rows)
                prob = probs[head, here, :].astype(F32)
                d_prob = dot(grad[here, cols], val, ((1,), (1,)))
                delta = jnp.sum(d_prob * prob, axis=1, keepdims=True)
                d_score[here, :] = (prob * (d_prob - delta)).astype(BF)
            dq = dot(d_score[...], key) * scale
            dk = dot(d_score[...], q, ((0,), (0,))) * scale
            dv = dot(probs[head], grad[:, cols], ((0,), (0,)))
            dq = turn(dq, cos_q, sin_q).astype(BF)
            dk = turn(dk, cos, sin).astype(BF)
            base = 0
            if shared:
                done[:, cols] = dq
                base = wide
            else:
                q_out[:, cols] = dq
            done[:, base + head * HEAD_DIM : base + (head + 1) * HEAD_DIM] = dk
            base += wide
            done[:, base + head * HEAD_DIM : base + (head + 1) * HEAD_DIM] = dv.astype(BF)
        for k in range(n_seq):
            at = pl.multiple_of(lax.rem(sc[1] + k, n_seq) * rows, rows)
            outs[k][...] = done[pl.ds(at, rows), :]

    ins = [sc] + chunks + ([] if shared else [queries]) + [kept, probs, cosine, sine]
    outs = [sds((rows, parts * wide), BF)] * n_seq
    if not shared:
        outs = [sds((rows, wide), BF)] + outs
    return call(
        body,
        ins,
        [SM] + [VM] * (len(ins) - 1),
        outs,
        [
            pltpu.VMEM((q_rows, wide), BF),
            pltpu.VMEM((frames, parts * wide), BF),
            pltpu.VMEM((q_rows, frames), BF),
        ],
        flops=8 * heads * q_rows * frames * HEAD_DIM,
        name="attend_backward",
    )


def project_backward(dims, layer, sc, chunks, w_own, w_other):
    rows, width, narrow, local, count = (
        dims.rows, dims.width, dims.narrow, dims.local, dims.n_heads,
    )
    n_seq = dims.n_seq
    n_in = len(chunks)

    def body(sc, *refs):
        chunks = refs[:n_in]
        w_own, w_other, d_out = refs[n_in : n_in + 3]
        outs = refs[n_in + 3 : n_in + 3 + count]
        weight, ready, buffer, sem = refs[n_in + 3 + count :]
        fetch = Fetch(sc, layer, w_own, w_other, weight, sem)
        if dims.spread_heads:
            wide = local // n_seq
            for k in range(n_seq):
                ready[lax.rem(sc[1] - k + n_seq, n_seq)] = chunks[k][...]
            grads = [
                jnp.concatenate(
                    [ready[j][:, p * wide : (p + 1) * wide] for j in range(n_seq)], axis=1
                )
                for p in range(3)
            ]
        else:
            total = chunks[1][...].astype(F32)
            for k in range(2, n_in):
                total = total + chunks[k][...].astype(F32)
            total = total.astype(BF)
            grads = [chunks[0][...], total[:, :local], total[:, local:]]
        for p in range(3):
            d_out[p] = grads[p]
        fetch.wait()
        total = dot(grads[0], weight[0], ((1,), (1,)))
        total = total + dot(grads[1], weight[1], ((1,), (1,)))
        total = total + dot(grads[2], weight[2], ((1,), (1,)))
        buffer[...] = total.astype(BF)
        hand_out(outs, buffer, sc[0], narrow)

    ready = (n_seq, rows, 3 * local // n_seq) if dims.spread_heads else (1, 8, 128)
    return call(
        body,
        [sc] + chunks + [w_own, w_other],
        [SM] + [VM] * n_in + [HB, HB],
        [sds((3, rows, local), BF)] + [sds((rows, narrow), BF)] * count,
        [
            pltpu.VMEM(w_own.shape, BF),
            pltpu.VMEM(ready, BF),
            pltpu.VMEM((rows, width), BF),
            pltpu.SemaphoreType.DMA,
        ],
        flops=6 * rows * width * local,
        name=f"project_backward_{layer}",
    )


def weight_grads(pairs, name):
    n = len(pairs)
    ins = [a for pair in pairs for a in pair]
    outs = []
    flops = 0
    for left, right in pairs:
        if right.ndim == 3:
            outs.append(sds((right.shape[0], left.shape[1], right.shape[2]), BF))
        else:
            outs.append(sds((left.shape[1], right.shape[1]), BF))
        flops += 2 * left.shape[0] * math.prod(outs[-1].shape)

    def body(*refs):
        for i in range(n):
            left, right, out = refs[2 * i], refs[2 * i + 1], refs[2 * n + i]
            if len(right.shape) == 3:
                for p in range(right.shape[0]):
                    out[p] = dot(left[...], right[p], ((0,), (0,))).astype(BF)
            else:
                out[...] = dot(left[...], right[...], ((0,), (0,))).astype(BF)

    return call(body, ins, [VM] * (2 * n), outs, flops=flops, name=name)


def split_sum(sc, tensors, others, n_seq):
    n = len(tensors)

    def rows_of(tensor):
        return tensor.shape[-2] // n_seq

    outs = []
    for tensor in tensors:
        shape = list(tensor.shape)
        shape[-2] = rows_of(tensor)
        outs += [sds(shape, BF)] * n_seq

    def body(sc, *refs):
        tensors, others, outs = refs[:n], refs[n : 2 * n], refs[2 * n :]
        for i in range(n):
            share = tensors[i].shape[-2] // n_seq
            for k in range(n_seq):
                at = pl.ds(pl.multiple_of(lax.rem(sc[1] + k, n_seq) * share, share), share)
                if len(tensors[i].shape) == 3:
                    total = tensors[i][:, at, :].astype(F32) + others[i][:, at, :].astype(F32)
                else:
                    total = tensors[i][at, :].astype(F32) + others[i][at, :].astype(F32)
                outs[i * n_seq + k][...] = total.astype(BF)

    flat = call(body, [sc] + tensors + others, [SM] + [VM] * (2 * n), outs, name="split_sum")
    return [flat[i * n_seq : (i + 1) * n_seq] for i in range(n)]


def assemble(sc, shares, shapes, n_seq):
    n = len(shapes)
    flat = [share for layer in shares for tensor in layer for share in tensor]

    def body(sc, *refs):
        outs = refs[2 * n * n_seq :]
        for layer in range(2):

            @pl.when(sc[2] == layer)
            def _(layer=layer):
                for i in range(n):
                    for k in range(n_seq):
                        share = refs[(layer * n + i) * n_seq + k]
                        size = share.shape[-2]
                        at = pl.ds(
                            pl.multiple_of(lax.rem(sc[1] - k + n_seq, n_seq) * size, size), size
                        )
                        if len(share.shape) == 3:
                            outs[i][:, at, :] = share[...].astype(F32)
                        else:
                            outs[i][at, :] = share[...].astype(F32)

    return call(
        body,
        [sc] + flat,
        [SM] + [VM] * len(flat),
        [sds(shape, F32) for shape in shapes],
        limit=40,
        name="assemble",
    )


def gate_sums(dims, layer, sc, g, x1, z, mod):
    rows, narrow, count = dims.rows, dims.narrow, dims.n_heads

    def body(sc, g, x1, z, mod, small, *shown):
        seg = segments(sc, (rows, 1), 0, sc[1] * rows)
        mine = lanes_of(sc[0], count, narrow)
        value = z[...].astype(F32)
        small[...] = utterance_sums(g[:, mine].astype(F32) * value, seg)
        if shown:
            gate = spread_narrow(mod, sc, layer, 5, seg, mine)
            shown[0][...] = (x1[:, mine] + gate * value).astype(BF)

    outs = [sds((4, narrow), F32)]
    if layer == 1:
        outs.append(sds((rows, narrow), BF))
    return call(body, [sc, g, x1, z, mod], [SM] + [VM] * 4, outs, name=f"gate_sums_{layer}")


def last_norm(dims, sc, terms, x, mod):
    rows, narrow, count = dims.rows, dims.narrow, dims.n_heads

    def body(sc, *refs):
        terms = refs[:count]
        x, mod, total_out, normed_out, inv_out, small, rows_out, buffer = refs[count:]
        seg = segments(sc, (rows, 1), 0, sc[1] * rows)
        mine = lanes_of(sc[0], count, narrow)
        total = terms[0][...].astype(F32)
        for term in terms[1:]:
            total = total + term[...].astype(F32)
        normed, inv = norm_of(x[...].astype(F32))
        buffer[...] = normed
        normed = buffer[:, mine]
        small[0] = utterance_sums(total, seg)
        small[1] = utterance_sums(total * normed, seg)
        scale = spread_narrow(mod, sc, 0, 1, seg, mine)
        grad = total * (1.0 + scale)
        total_out[...] = grad
        normed_out[...] = normed
        inv_out[...] = inv
        rows_out[...] = jnp.concatenate(
            [jnp.sum(grad, axis=1, keepdims=True), jnp.sum(grad * normed, axis=1, keepdims=True)],
            axis=1,
        )

    return call(
        body,
        [sc] + terms + [x, mod],
        [SM] + [VM] * (count + 2),
        [
            sds((rows, narrow), F32),
            sds((rows, narrow), F32),
            sds((rows, 1), F32),
            sds((2, 4, narrow), F32),
            sds((rows, 2), F32),
        ],
        [pltpu.VMEM((rows, dims.width), F32)],
        name="last_norm",
    )


def last_pull(dims, sc, d_mid, grad, normed, inv, sums):
    rows, narrow, count, width = dims.rows, dims.narrow, dims.n_heads, dims.width

    def body(sc, d_mid, grad, normed, inv, *refs):
        sums, out = refs[:count], refs[count]
        total = sums[0][...]
        for term in sums[1:]:
            total = total + term[...]
        total = total * (1.0 / width)
        mine = lanes_of(sc[0], count, narrow)
        out[...] = d_mid[:, mine] + inv[...] * (
            grad[...] - total[:, 0:1] - normed[...] * total[:, 1:2]
        )

    return call(
        body,
        [sc, d_mid, grad, normed, inv] + sums,
        [SM] + [VM] * (4 + count),
        [sds((rows, narrow), F32)],
        name="last_pull",
    )[0]


def modulation_grads(sc, act, mod_weight, own, other, n_seq):
    kinds, width, narrow = mod_weight.shape

    def body(sc, act, mod_weight, *refs):
        own, other = refs[:n_seq], refs[n_seq : 2 * n_seq]
        g_mod, part, box = refs[2 * n_seq :]
        for k in range(n_seq):
            at = lax.rem(sc[1] - k + n_seq, n_seq)
            box[at, sc[2]] = own[k][...]
            box[at, 1 - sc[2]] = other[k][...]
        total = box[0]
        for j in range(1, n_seq):
            total = total + box[j]
        act_now = act[...]
        result = jnp.zeros((8, width), F32)
        for which in range(kinds):
            rows = jnp.concatenate([total[0, which], total[1, which]], axis=0)
            g_mod[which] = exact_outer(act_now, rows)
            result = result + exact_dot(rows, mod_weight[which], ((1,), (1,)))
        part[...] = result

    return call(
        body,
        [sc, act, mod_weight] + own + other,
        [SM] + [VM] * (2 + 2 * n_seq),
        [sds((kinds, width, narrow), F32), sds((8, width), F32)],
        [pltpu.VMEM((n_seq, 2, kinds, 4, narrow), F32)],
        limit=40,
        flops=2 * 64 * 3_000_000,
        name="modulation_grads",
    )


def time_backward(sc, sinus, inner, outer, time_out, own, other):
    count = len(own)
    rows, width = inner.shape

    def body(sc, sinus, inner, outer, time_out, *refs):
        own, other = refs[:count], refs[count : 2 * count]
        g_in, g_out, box = refs[2 * count :]
        for k in range(count):
            at = lax.rem(sc[0] - k + count, count)
            box[at, sc[2]] = own[k][...]
            box[at, 1 - sc[2]] = other[k][...]
        total = jnp.zeros((rows, width), F32)
        for j in range(count):
            for c in range(2):
                total = total + box[j, c]

        def slope(value):
            gate = 1.0 / (1.0 + jnp.exp(-value))
            return gate * (1.0 + value * (1.0 - gate))

        pre = inner[...]
        hidden = pre / (1.0 + jnp.exp(-pre))
        d_outer = total * slope(outer[...])
        g_out[...] = exact_outer(hidden, d_outer)
        d_inner = exact_dot(d_outer, time_out[...], ((1,), (1,))) * slope(pre)
        g_in[...] = exact_outer(sinus[...], d_inner)

    return call(
        body,
        [sc, sinus, inner, outer, time_out] + own + other,
        [SM] + [VM] * (4 + 2 * count),
        [sds((sinus.shape[1], width), F32), sds((width, width), F32)],
        [pltpu.VMEM((count, 2, rows, width), F32)],
        flops=2 * 64 * 1_500_000,
        name="time_backward",
    )


class Dims:
    pass


def local_program(
    frames,
    cotangent,
    utt_lengths,
    time_ids,
    w_time_in,
    w_time_out,
    w_mod,
    w_qkv,
    w_out,
    w_up,
    w_down,
):
    micro_count, rows, narrow = frames.shape
    dims = Dims()
    dims.n_heads = lax.axis_size("heads")
    dims.n_seq = n_seq = lax.axis_size("seq")
    dims.rows, dims.narrow = rows, narrow
    dims.width = narrow * dims.n_heads
    dims.local = w_qkv.shape[3]
    dims.hidden = w_up.shape[2]
    dims.frames = rows * n_seq
    heads_local = dims.local // HEAD_DIM
    dims.spread_heads = heads_local % n_seq == 0
    dims.heads_here = heads_local // n_seq if dims.spread_heads else heads_local
    dims.n_chunks = n_seq if dims.spread_heads else 2
    at_heads = lax.axis_index("heads")
    at_seq = lax.axis_index("seq")
    section = lax.axis_index("section")

    lengths = lax.dynamic_index_in_dim(utt_lengths, section, 0, keepdims=False)
    sc = jnp.stack(
        [at_heads, at_seq, section, lengths[0], lengths[0] + lengths[1]]
    ).astype(jnp.int32)

    qkv = jnp.transpose(w_qkv[0], (1, 0, 2))
    mod_weight = jnp.transpose(w_mod[0], (1, 0, 2))
    own_weights = (qkv, w_out[0], w_up[0], w_down[0])
    wide_frames = gather(
        lax.dynamic_index_in_dim(frames, section, 0, keepdims=False), "heads"
    )
    qkv_w, out_w, up_w, down_w = [(w, swap(w)) for w in own_weights]
    wide_cotangent = gather(
        lax.dynamic_index_in_dim(cotangent, section, 0, keepdims=False), "heads"
    )

    index = jnp.arange(dims.frames, dtype=jnp.int32)
    begin = jnp.where(index >= sc[4], sc[4], jnp.where(index >= sc[3], sc[3], 0))
    position = (index - begin).astype(F32)
    lane = np.arange(2 * HEAD_DIM)
    rate = np.exp(
        np.arange(HEAD_DIM // 2, dtype=np.float32)
        * np.float32(-2.0 * math.log(10000.0) / HEAD_DIM)
    ).astype(np.float32)[(lane % HEAD_DIM) // 2]
    angle = position[:, None] * jnp.asarray(rate)[None, :]
    cosine = jnp.cos(angle)
    sine = jnp.sin(angle) * jnp.asarray(np.where(lane % 2 == 0, -1.0, 1.0), F32)[None, :]

    half = FREQ // 2
    frequency = jnp.exp(jnp.arange(half, dtype=F32) * (-math.log(10000.0) / (half - 1)))
    angle_t = time_ids.astype(F32)[..., None] * frequency
    sinus = jnp.concatenate([jnp.sin(angle_t), jnp.cos(angle_t)], axis=-1)
    sinus = jnp.pad(sinus, ((0, 0), (0, 1), (0, 0))).reshape(micro_count * 4, FREQ)
    inner, outer, act, modul = time_forward(sinus, w_time_in, w_time_out, mod_weight)
    mod = collect_modulation(sc, gather(modul, "heads"), pair_gather(modul, "heads"))

    saved = []
    pieces = wide_frames
    for layer in range(2):
        x, x_narrow, xa, *sent = project(
            dims, layer, sc, pieces, mod, *qkv_w, cosine, sine
        )
        if dims.spread_heads:
            queries = None
            kept, probs, *mixed = attend(dims, sc, exchange(sent, "seq"), None)
            mixed = exchange(mixed, "seq")
        else:
            queries = sent[0]
            kept, probs, *mixed = attend(dims, sc, gather(sent[1], "seq"), queries)
        att, *terms = project_out(dims, layer, sc, mixed, *out_w)
        branch = gather(add_chunks(exchange(terms, "heads")), "heads")
        x1, xf, h, slope, *terms = feed_forward(dims, layer, sc, x, branch, mod, up_w, down_w)
        if layer == 0:
            z = gather(add_chunks(exchange(terms, "heads")), "heads")
            pieces = [x1] + z
        else:
            z = [terms]
        saved.append(
            dict(x=x, x_narrow=x_narrow, xa=xa, kept=kept, probs=probs, queries=queries, att=att,
                 branch=branch[0], x1=x1, xf=xf, h=h, slope=slope, z=z[0])
        )

    shares = [None, None]
    small = [None, None]
    pieces = wide_cotangent
    for layer in (1, 0):
        now = saved[layer]
        g, dz, da, *rest = feed_backward(
            dims, layer, sc, pieces, now["slope"], mod, up_w, down_w
        )
        terms, rest = rest[: dims.n_heads], rest[dims.n_heads :]
        if layer == 0:
            middle_grad, small_a1 = rest
        sums = gather(add_chunks(exchange(terms, "heads")), "heads")
        if layer == 1:
            z_terms = now["z"]
            z_now = add_chunks(exchange(z_terms, "heads"))
        else:
            z_now = now["z"]
        gate_small, *shown_last = gate_sums(dims, layer, sc, g, now["x1"], z_now, mod)
        if layer == 1:
            shown = shown_last[0]
        g_down, g_up = weight_grads([(now["h"], dz), (now["xf"], da)], f"feed_grads_{layer}")
        d_mid, dy, small_f, *sent = middle_backward(
            dims, layer, sc, g, now["x1"], sums, now["branch"], mod, *out_w
        )
        (g_out,) = weight_grads([(now["att"], dy)], f"out_grad_{layer}")
        if dims.spread_heads:
            sent = exchange(sent, "seq")
        sent = attend_backward(
            dims, sc, sent, now["queries"], now["kept"], now["probs"], cosine, sine
        )
        if dims.spread_heads:
            sent = exchange(sent, "seq")
        else:
            sent = [sent[0]] + exchange(sent[1:], "seq")
        d_qkv, *terms = project_backward(dims, layer, sc, sent, *qkv_w)
        (g_qkv,) = weight_grads([(now["xa"], d_qkv)], f"qkv_grad_{layer}")
        if layer == 1:
            pieces = gather(add_chunks(exchange(terms, "heads")), "heads") + [now["x"], d_mid]
        else:
            terms = exchange(terms, "heads")
        small[layer] = (gate_small, small_f)
        done = []
        for group in ([g_down, g_up], [g_out], [g_qkv]):
            parts = split_sum(sc, group, [swap(g) for g in group], n_seq)
            for part in parts:
                total = add_chunks([owner_shift(p, layer, k) for k, p in enumerate(part)])
                done.append([owner_shift(total, layer, k) for k in range(n_seq)])
        shares[layer] = done

    grad, normed, inv, small_a0, row_sums = last_norm(dims, sc, terms, saved[0]["x"], mod)
    first_grad = last_pull(dims, sc, d_mid, grad, normed, inv, gather(row_sums, "heads"))

    def stack(layer, small_a):
        gate, mid = small[layer]
        return jnp.concatenate([small_a, mid, gate[None]], axis=0)

    by_layer = jnp.stack([stack(0, small_a0), stack(1, small_a1)])
    own_layer = lax.dynamic_index_in_dim(by_layer, section, 0, keepdims=False)
    other_layer = lax.dynamic_index_in_dim(by_layer, 1 - section, 0, keepdims=False)
    g_mod, part = modulation_grads(
        sc, act, mod_weight, gather(own_layer, "seq"), pair_gather(other_layer, "seq"), n_seq
    )
    g_first, g_second = time_backward(
        sc, sinus, inner, outer, w_time_out, gather(part, "heads"), pair_gather(part, "heads")
    )

    shapes = [w_down.shape[1:], w_up.shape[1:], w_out.shape[1:], qkv.shape]
    outs = []
    for picked in ((0, 1), (2,), (3,)):
        outs += assemble(
            sc,
            [[shares[layer][i] for i in picked] for layer in range(2)],
            [shapes[i] for i in picked],
            n_seq,
        )
    g_reduce, g_expand, g_out, g_qkv = outs

    def relaid(layer_0, layer_1):
        own = jnp.where(section == 0, layer_0, layer_1)
        other = swap(jnp.where(section == 0, layer_1, layer_0))
        return jnp.where(section == 0, jnp.stack([own, other]), jnp.stack([other, own]))[None]

    acts = relaid(saved[1]["x_narrow"], shown)
    grads = relaid(first_grad, middle_grad)
    return (
        acts,
        grads,
        g_first,
        g_second,
        jnp.transpose(g_mod, (1, 0, 2))[None],
        jnp.transpose(g_qkv, (1, 0, 2))[None],
        g_out[None],
        g_expand[None],
        g_reduce[None],
    )


def solution(mesh):
    placed = (
        P(None, "seq", "heads"),
        P(None, "seq", "heads"),
        P(),
        P(),
        P(),
        P(),
        P("section", None, None, "heads"),
        P("section", None, None, "heads"),
        P("section", "heads", None),
        P("section", None, "heads"),
        P("section", "heads", None),
    )
    return jax.shard_map(
        local_program,
        mesh=mesh,
        in_specs=placed,
        out_specs=(
            P("section", None, "seq", "heads"),
            P("section", None, "seq", "heads"),
            P(),
            P(),
            P("section", None, None, "heads"),
            P("section", None, None, "heads"),
            P("section", "heads", None),
            P("section", None, "heads"),
            P("section", "heads", None),
        ),
        check_vma=False,
    )
```

time: 1650 us -> 507 us (0.31)
  blocking collectives: 619 us -> 0 us
  matrix products: 231 us -> 0 us
  starting transfers between devices: 10.4 us -> 237 us
  waiting for transfers between devices: 350 us -> 148 us
  local copies, waits for them, and re-layouts: 227 us -> 30.8 us
  other arithmetic: 156 us -> 7.76 us
  Pallas kernels: 0 us -> 68.9 us
  loops' own time: 17.6 us -> 0 us
    all_gather x30 -> x0, blocking collectives: 410 us -> none  [the longest x12 175 us: widen(): return lax.all_gather(narrow_part, 'heads', axis=1, tiled=True)]
    reduce_scatter x21 -> x0, waiting for transfers between devices: 243 us -> none  [the longest x12 117 us: reduce_heads(): lax.psum_scatter(term.astype(jnp.bfloat16), 'heads', scatter_dimension=1,...]
    dot_general x131 -> x0, matrix products: 231 us -> none  [the longest x62 85.9 us: exact(): return jnp.einsum(spec, left, right, precision=lax.Precision.HIGHEST)]
    ppermute x6 -> x158, starting transfers between devices: 9.61 us -> 237 us  [the longest x84 111 us: shifted(): lax.ppermute(value, axis, [(i, (i + by) % length) for i in range(length)])]
    psum x19 -> x0, blocking collectives: 209 us -> none  [the longest x18 170 us: across_heads(): return lax.psum((first_sum, second_sum), 'heads')]
    ppermute x6 -> x158, waiting for transfers between devices: 1.87 us -> 148 us  [the longest x84 116 us: shifted(): lax.ppermute(value, axis, [(i, (i + by) % length) for i in range(length)])]
    psum x1 -> x0, waiting for transfers between devices: 104 us -> none  [local(): lax.psum(g_mod_local.astype(jnp.bfloat16), 'seq').astype(jnp.float32)]
    pallas_call x0 -> x39, Pallas kernels: none -> 68.9 us  [call(): pl.pallas_call(body, out_shape=list(outs), in_specs=list(specs), out_spec...]
  transfers between devices with their start and end apart: 28 -> 158, of which waited for: 22 -> 75; matrix products, arithmetic and copies ran while one was open for 8% -> 2% of each run, Pallas kernels for 0% -> 9%
where the time goes in v1:
time: 507 us; the launch traced here: 497 us
  starting transfers between devices  237 us (47%)
  waiting for transfers between devices  148 us (29%)
  Pallas kernels  68.9 us (14%)
  local copies, waits for them, and re-layouts  30.8 us (6%)
  other arithmetic  7.76 us (2%)
    ppermute x84, waiting for transfers between devices, shifted(): lax.ppermute(value, axis, [(i, (i + by) % length) for i in range(length)])  116 us
    ppermute x84, starting transfers between devices, shifted(): lax.ppermute(value, axis, [(i, (i + by) % length) for i in range(length)])  111 us
    ppermute x48, starting transfers between devices, owner_shift(): return lax.ppermute(value, ('section', 'seq'), pairs)  98.6 us
    pallas_call x39, Pallas kernels, call(): pl.pallas_call(body, out_shape=list(outs), in_specs=list(specs), out_spec...  68.9 us
    unnamed x214, local copies, waits for them, and re-layouts  28.8 us
    ppermute x48, waiting for transfers between devices, owner_shift(): return lax.ppermute(value, ('section', 'seq'), pairs)  26.2 us
    ppermute x12, starting transfers between devices, pair_shift(): return lax.ppermute(value, ('section', axis), pairs)  14.9 us
    ppermute x14, starting transfers between devices, swap(): return lax.ppermute(value, 'section', [(0, 1), (1, 0)])  12.6 us
  transfers between devices with their start and end apart: 158, of which 75 were waited for; matrix products, arithmetic and copies ran while one was open for 2% of the time, Pallas kernels for 9%

profile of v1, /device:TPU:0, one launch (start us, length us, event | category | flops | bytes accessed | tf_op | source)
XLA Modules:
  0.0 497.1 jit_solution(18358120489634450144)
XLA Ops:
  9.6 4.7 collective-permute-start.9
  31.0 4.5 collective-permute-done.1.refs_2_
  83.6 3.8 collective-permute-start.23
  155.5 4.2 collective-permute-done.45.refs_2_
  175.5 3.9 collective-permute-start.56
  220.5 8.1 %collective-permute-done.67.refs_2_ = bf16[176,256]{1,0:T(8,128)(2,1)S(1)} collective-permute-done((bf16[176,256]{1,0:T(8,128)(2,1)S(1)}, bf16[176,256]{1,0:T(8,128)(2,1)S(1)}, u32[]{:S(2)}, u32[]{:S(2)}) %collective-permute-start.67) | collective-permute-done | bytes 90144 | tf_op jit(solution)/shard_map/ppermute | solution.py:24
  283.3 5.2 %collective-permute-done.81.refs_1_ = bf16[176,256]{1,0:T(8,128)(2,1)S(1)} collective-permute-done((bf16[176,256]{1,0:T(8,128)(2,1)S(1)}, bf16[176,256]{1,0:T(8,128)(2,1)S(1)}, u32[]{:S(2)}, u32[]{:S(2)}) %collective-permute-start.81) | collective-permute-done | bytes 90144 | tf_op jit(solution)/shard_map/ppermute | solution.py:24
  299.6 4.5 collective-permute-done.85.refs_2_
  316.4 5.1 %modulation_grads.1 = (f32[6,1024,256]{2,1,0:T(8,128)}, f32[8,1024]{1,0:T(8,128)S(1)}) custom-call(s32[5]{0:T(128)S(1)} %stack.56.sc, f32[8,1024]{1,0:T(8,128)S(1)} %copy-done.77, bf16[6,1024,256]{2,1,0:T(8,128)(2,1)S(1)} %bitcast.66, f32[6,4,256]{2,1,0:T(4,128)S(1)} %get-tuple-element.318.refs_0_, f32[6,4,256]{2,1,0:T(4,128)S(1)} %collective-permute-done.88.refs_1_, ...), custom_call_target="tpu_custom_call" | custom-call | flops 384000000 | bytes 9699348 | tf_op jit(solution)/shard_map/modulation_grads/pallas_call | solution.py:195
  321.5 6.5 %collective-permute-start.101 = (f32[8,1024]{1,0:T(8,128)S(1)}, f32[8,1024]{1,0:T(8,128)S(1)}, u32[]{:S(2)}, u32[]{:S(2)}) collective-permute-start(f32[8,1024]{1,0:T(8,128)S(1)} %get-tuple-element.255.refs_0_), channel_id=1, source_target_pairs={{0,19},{1,16},{2,17},{3,18},{16,3},{17,0},{18,1},{19,2},{4,23},{5,... | collective-permute-start | bytes 98312 | tf_op jit(solution)/shard_map/ppermute | solution.py:42
  336.8 4.0 collective-permute-done.96.refs_2_
  356.2 4.3 collective-permute-start.119
  370.3 4.4 collective-permute-start.102
  377.8 3.9 collective-permute-done.122.refs_3_
  384.3 4.2 collective-permute-done.121.refs_2_
  388.5 6.3 %collective-permute-start.120 = (bf16[64,1024]{1,0:T(8,128)(2,1)S(1)}, bf16[64,1024]{1,0:T(8,128)(2,1)S(1)}, u32[]{:S(2)}, u32[]{:S(2)}) collective-permute-start(bf16[64,1024]{1,0:T(8,128)(2,1)S(1)} %add_convert_fusion.7.refs_0_), channel_id=1, source_target_pairs={{0,4},{4,8},{8,12},{12,0},{1,5},{5,9},{9,13},{13,1},{2,6},{6,10},{... | collective-permute-start | bytes 393224 | tf_op jit(solution)/shard_map/ppermute | solution.py:59
  395.0 4.1 collective-permute-done.120.refs_1_
  410.6 3.9 collective-permute-start.134
  418.1 6.9 %collective-permute-done.133 = bf16[128,1024]{1,0:T(8,128)(2,1)S(1)} collective-permute-done((bf16[128,1024]{1,0:T(8,128)(2,1)S(1)}, bf16[128,1024]{1,0:T(8,128)(2,1)S(1)}, u32[]{:S(2)}, u32[]{:S(2)}) %collective-permute-start.133) | collective-permute-done | bytes 262176 | tf_op jit(solution)/shard_map/ppermute | solution.py:59
  435.8 10.8 %collective-permute-start.137 = (bf16[128,1024]{1,0:T(8,128)(2,1)S(1)}, bf16[128,1024]{1,0:T(8,128)(2,1)S(1)}, u32[]{:S(2)}, u32[]{:S(2)}) collective-permute-start(bf16[128,1024]{1,0:T(8,128)(2,1)S(1)} %add_convert_fusion.5.refs_0_), channel_id=1, source_target_pairs={{0,12},{4,0},{8,4},{12,8},{1,13},{5,1},{9,5},{13,9},{2,14},{6,2},{... | collective-permute-start | bytes 786440 | tf_op jit(solution)/shard_map/ppermute | solution.py:59
  454.4 4.8 collective-permute-start.105
  462.4 4.8 collective-permute-start.143
  475.5 3.7 collective-permute-start.108
  484.9 4.0 time_backward.1
  (579 shorter events, 371.7 us)
Async XLA Ops:
  0.7 44.1 %collective-permute-start.10 = (bf16[3,1024,256]{2,1,0:T(8,128)(2,1)}, bf16[3,1024,256]{2,1,0:T(8,128)(2,1)S(1)}, u32[]{:S(2)}, u32[]{:S(2)}) collective-permute-start(bf16[3,1024,256]{2,1,0:T(8,128)(2,1)} %bitcast.45), channel_id=1, source_target_pairs={{0,16},{16,0},{1,17},{17,1},{2,18},{18,2},{3,19},{19,3},{4,20},{20... | collective-permute-start | bytes 4718600 | tf_op jit(solution)/shard_map/ppermute | solution.py:50
  24.5 63.5 %collective-permute-start.24 = (bf16[1024,512]{1,0:T(8,128)(2,1)}, bf16[1024,512]{1,0:T(8,128)(2,1)}, u32[]{:S(2)}, u32[]{:S(2)}) collective-permute-start(bf16[1024,512]{1,0:T(8,128)(2,1)} %bitcast.50), channel_id=1, source_target_pairs={{0,16},{16,0},{1,17},{17,1},{2,18},{18,2},{3,19},{19,3},{4,20},{20... | collective-permute-start | bytes 3145736 | tf_op jit(solution)/shard_map/ppermute | solution.py:50
  25.4 62.6 %collective-permute-start.25 = (bf16[512,1024]{1,0:T(8,128)(2,1)}, bf16[512,1024]{1,0:T(8,128)(2,1)}, u32[]{:S(2)}, u32[]{:S(2)}) collective-permute-start(bf16[512,1024]{1,0:T(8,128)(2,1)} %bitcast.55), channel_id=1, source_target_pairs={{0,16},{16,0},{1,17},{17,1},{2,18},{18,2},{3,19},{19,3},{4,20},{20... | collective-permute-start | bytes 3145736 | tf_op jit(solution)/shard_map/ppermute | solution.py:50
  30.3 38.9 %collective-permute-start.17 = (bf16[256,1024]{1,0:T(8,128)(2,1)}, bf16[256,1024]{1,0:T(8,128)(2,1)}, u32[]{:S(2)}, u32[]{:S(2)}) collective-permute-start(bf16[256,1024]{1,0:T(8,128)(2,1)} %bitcast.60), channel_id=1, source_target_pairs={{0,16},{16,0},{1,17},{17,1},{2,18},{18,2},{3,19},{19,3},{4,20},{20... | collective-permute-start | bytes 1572872 | tf_op jit(solution)/shard_map/ppermute | solution.py:50
  242.8 29.6 %collective-permute-start.47 = (bf16[176,256]{1,0:T(8,128)(2,1)}, bf16[176,256]{1,0:T(8,128)(2,1)}, u32[]{:S(2)}, u32[]{:S(2)}) collective-permute-start(bf16[176,256]{1,0:T(8,128)(2,1)} %get-tuple-element.198), channel_id=1, source_target_pairs={{0,1},{1,2},{2,3},{3,0},{4,5},{5,6},{6,7},{7,4},{8,9},{9,10},{10,1... | collective-permute-start | bytes 270344 | tf_op jit(solution)/shard_map/ppermute | solution.py:24
  245.6 27.7 %collective-permute-start.48 = (bf16[176,256]{1,0:T(8,128)(2,1)}, bf16[176,256]{1,0:T(8,128)(2,1)}, u32[]{:S(2)}, u32[]{:S(2)}) collective-permute-start(bf16[176,256]{1,0:T(8,128)(2,1)} %get-tuple-element.199), channel_id=1, source_target_pairs={{0,2},{1,3},{2,0},{3,1},{4,6},{5,7},{6,4},{7,5},{8,10},{9,11},{10,... | collective-permute-start | bytes 270344 | tf_op jit(solution)/shard_map/ppermute | solution.py:24
  246.7 27.4 %collective-permute-start.49 = (bf16[176,256]{1,0:T(8,128)(2,1)}, bf16[176,256]{1,0:T(8,128)(2,1)}, u32[]{:S(2)}, u32[]{:S(2)}) collective-permute-start(bf16[176,256]{1,0:T(8,128)(2,1)} %get-tuple-element.200), channel_id=1, source_target_pairs={{0,3},{1,0},{2,1},{3,2},{4,7},{5,4},{6,5},{7,6},{8,11},{9,8},{10,9... | collective-permute-start | bytes 270344 | tf_op jit(solution)/shard_map/ppermute | solution.py:24
  266.6 76.5 %collective-permute-start.144 = (bf16[512,1024]{1,0:T(8,128)(2,1)S(1)}, bf16[512,1024]{1,0:T(8,128)(2,1)S(1)}, u32[]{:S(2)}, u32[]{:S(2)}) collective-permute-start(bf16[512,1024]{1,0:T(8,128)(2,1)S(1)} %get-tuple-element.301.refs_0_), channel_id=1, source_target_pairs={{0,16},{16,0},{1,17},{17,1},{2,18},{18,2},{3,19},{19,3},{4,20},{20... | collective-permute-start | bytes 3145736 | tf_op jit(solution)/shard_map/ppermute | solution.py:50
  266.7 81.3 %collective-permute-start.145 = (bf16[1024,512]{1,0:T(8,128)(2,1)S(1)}, bf16[1024,512]{1,0:T(8,128)(2,1)S(1)}, u32[]{:S(2)}, u32[]{:S(2)}) collective-permute-start(bf16[1024,512]{1,0:T(8,128)(2,1)S(1)} %get-tuple-element.302.refs_1_), channel_id=1, source_target_pairs={{0,16},{16,0},{1,17},{17,1},{2,18},{18,2},{3,19},{19,3},{4,20},{20... | collective-permute-start | bytes 3145736 | tf_op jit(solution)/shard_map/ppermute | solution.py:50
  278.8 17.3 %collective-permute-start.123 = (bf16[256,1024]{1,0:T(8,128)(2,1)S(1)}, bf16[256,1024]{1,0:T(8,128)(2,1)S(1)}, u32[]{:S(2)}, u32[]{:S(2)}) collective-permute-start(bf16[256,1024]{1,0:T(8,128)(2,1)S(1)} %out_grad_1.1.refs_0_), channel_id=1, source_target_pairs={{0,16},{16,0},{1,17},{17,1},{2,18},{18,2},{3,19},{19,3},{4,20},{20... | collective-permute-start | bytes 1572872 | tf_op jit(solution)/shard_map/ppermute | solution.py:50
  364.3 35.5 %collective-permute-start.130 = (bf16[512,1024]{1,0:T(8,128)(2,1)S(1)}, bf16[512,1024]{1,0:T(8,128)(2,1)S(1)}, u32[]{:S(2)}, u32[]{:S(2)}) collective-permute-start(bf16[512,1024]{1,0:T(8,128)(2,1)S(1)} %get-tuple-element.287.refs_0_), channel_id=1, source_target_pairs={{0,16},{16,0},{1,17},{17,1},{2,18},{18,2},{3,19},{19,3},{4,20},{20... | collective-permute-start | bytes 3145736 | tf_op jit(solution)/shard_map/ppermute | solution.py:50
  365.4 35.1 %collective-permute-start.131 = (bf16[1024,512]{1,0:T(8,128)(2,1)S(1)}, bf16[1024,512]{1,0:T(8,128)(2,1)S(1)}, u32[]{:S(2)}, u32[]{:S(2)}) collective-permute-start(bf16[1024,512]{1,0:T(8,128)(2,1)S(1)} %get-tuple-element.288.refs_1_), channel_id=1, source_target_pairs={{0,16},{16,0},{1,17},{17,1},{2,18},{18,2},{3,19},{19,3},{4,20},{20... | collective-permute-start | bytes 3145736 | tf_op jit(solution)/shard_map/ppermute | solution.py:50
  366.8 47.7 %collective-permute-start.109 = (bf16[3,1024,256]{2,1,0:T(8,128)(2,1)S(1)}, bf16[3,1024,256]{2,1,0:T(8,128)(2,1)S(1)}, u32[]{:S(2)}, u32[]{:S(2)}) collective-permute-start(bf16[3,1024,256]{2,1,0:T(8,128)(2,1)S(1)} %qkv_grad_1.1.refs_0_), channel_id=1, source_target_pairs={{0,16},{16,0},{1,17},{17,1},{2,18},{18,2},{3,19},{19,3},{4,20},{20... | collective-permute-start | bytes 4718600 | tf_op jit(solution)/shard_map/ppermute | solution.py:50
  370.3 60.4 %collective-permute-start.102 = (bf16[3,1024,256]{2,1,0:T(8,128)(2,1)S(1)}, bf16[3,1024,256]{2,1,0:T(8,128)(2,1)S(1)}, u32[]{:S(2)}, u32[]{:S(2)}) collective-permute-start(bf16[3,1024,256]{2,1,0:T(8,128)(2,1)S(1)} %qkv_grad_0.1.refs_0_), channel_id=1, source_target_pairs={{0,16},{16,0},{1,17},{17,1},{2,18},{18,2},{3,19},{19,3},{4,20},{20... | collective-permute-start | bytes 4718600 | tf_op jit(solution)/shard_map/ppermute | solution.py:50
  407.3 17.7 %collective-permute-start.133 = (bf16[128,1024]{1,0:T(8,128)(2,1)S(1)}, bf16[128,1024]{1,0:T(8,128)(2,1)S(1)}, u32[]{:S(2)}, u32[]{:S(2)}) collective-permute-start(bf16[128,1024]{1,0:T(8,128)(2,1)S(1)} %get-tuple-element.291), channel_id=1, source_target_pairs={{0,8},{4,12},{8,0},{12,4},{1,9},{5,13},{9,1},{13,5},{2,10},{6,14},... | collective-permute-start | bytes 786440 | tf_op jit(solution)/shard_map/ppermute | solution.py:59
  417.4 31.6 %collective-permute-start.110 = (bf16[3,256,256]{2,1,0:T(8,128)(2,1)S(1)}, bf16[3,256,256]{2,1,0:T(8,128)(2,1)S(1)}, u32[]{:S(2)}, u32[]{:S(2)}) collective-permute-start(bf16[3,256,256]{2,1,0:T(8,128)(2,1)S(1)} %get-tuple-element.268), channel_id=1, source_target_pairs={{16,20},{20,24},{24,28},{28,16},{17,21},{21,25},{25,29},{29,17},{1... | collective-permute-start | bytes 1179656 | tf_op jit(solution)/shard_map/ppermute | solution.py:59
  425.0 26.0 %collective-permute-start.111 = (bf16[3,256,256]{2,1,0:T(8,128)(2,1)S(1)}, bf16[3,256,256]{2,1,0:T(8,128)(2,1)S(1)}, u32[]{:S(2)}, u32[]{:S(2)}) collective-permute-start(bf16[3,256,256]{2,1,0:T(8,128)(2,1)S(1)} %get-tuple-element.269), channel_id=1, source_target_pairs={{16,24},{20,28},{24,16},{28,20},{17,25},{21,29},{25,17},{29,21},{1... | collective-permute-start | bytes 1179656 | tf_op jit(solution)/shard_map/ppermute | solution.py:59
  425.7 28.7 %collective-permute-start.112 = (bf16[3,256,256]{2,1,0:T(8,128)(2,1)S(1)}, bf16[3,256,256]{2,1,0:T(8,128)(2,1)S(1)}, u32[]{:S(2)}, u32[]{:S(2)}) collective-permute-start(bf16[3,256,256]{2,1,0:T(8,128)(2,1)S(1)} %get-tuple-element.270), channel_id=1, source_target_pairs={{16,28},{20,16},{24,20},{28,24},{17,29},{21,17},{25,21},{29,25},{1... | collective-permute-start | bytes 1179656 | tf_op jit(solution)/shard_map/ppermute | solution.py:59
  435.8 23.7 %collective-permute-start.137 = (bf16[128,1024]{1,0:T(8,128)(2,1)S(1)}, bf16[128,1024]{1,0:T(8,128)(2,1)S(1)}, u32[]{:S(2)}, u32[]{:S(2)}) collective-permute-start(bf16[128,1024]{1,0:T(8,128)(2,1)S(1)} %add_convert_fusion.5.refs_0_), channel_id=1, source_target_pairs={{0,12},{4,0},{8,4},{12,8},{1,13},{5,1},{9,5},{13,9},{2,14},{6,2},{... | collective-permute-start | bytes 786440 | tf_op jit(solution)/shard_map/ppermute | solution.py:59
  451.0 16.2 %collective-permute-start.104 = (bf16[3,256,256]{2,1,0:T(8,128)(2,1)S(1)}, bf16[3,256,256]{2,1,0:T(8,128)(2,1)S(1)}, u32[]{:S(2)}, u32[]{:S(2)}) collective-permute-start(bf16[3,256,256]{2,1,0:T(8,128)(2,1)S(1)} %get-tuple-element.263), channel_id=1, source_target_pairs={{0,8},{4,12},{8,0},{12,4},{1,9},{5,13},{9,1},{13,5},{2,10},{6,14},... | collective-permute-start | bytes 1179656 | tf_op jit(solution)/shard_map/ppermute | solution.py:59
  459.5 22.8 %collective-permute-start.115 = (bf16[3,256,256]{2,1,0:T(8,128)(2,1)S(1)}, bf16[3,256,256]{2,1,0:T(8,128)(2,1)S(1)}, u32[]{:S(2)}, u32[]{:S(2)}) collective-permute-start(bf16[3,256,256]{2,1,0:T(8,128)(2,1)S(1)} %add_convert_fusion.refs_4_), channel_id=1, source_target_pairs={{16,28},{20,16},{24,20},{28,24},{17,29},{21,17},{25,21},{29,25},{1... | collective-permute-start | bytes 1179656 | tf_op jit(solution)/shard_map/ppermute | solution.py:59
  471.9 22.3 %collective-permute-start.114 = (bf16[3,256,256]{2,1,0:T(8,128)(2,1)S(1)}, bf16[3,256,256]{2,1,0:T(8,128)(2,1)S(1)}, u32[]{:S(2)}, u32[]{:S(2)}) collective-permute-start(bf16[3,256,256]{2,1,0:T(8,128)(2,1)S(1)} %add_convert_fusion.refs_4_), channel_id=1, source_target_pairs={{16,24},{20,28},{24,16},{28,20},{17,25},{21,29},{25,17},{29,21},{1... | collective-permute-start | bytes 1179656 | tf_op jit(solution)/shard_map/ppermute | solution.py:59
  472.9 21.3 %collective-permute-start.113 = (bf16[3,256,256]{2,1,0:T(8,128)(2,1)S(1)}, bf16[3,256,256]{2,1,0:T(8,128)(2,1)S(1)}, u32[]{:S(2)}, u32[]{:S(2)}) collective-permute-start(bf16[3,256,256]{2,1,0:T(8,128)(2,1)S(1)} %add_convert_fusion.refs_4_), channel_id=1, source_target_pairs={{16,20},{20,24},{24,28},{28,16},{17,21},{21,25},{25,29},{29,17},{1... | collective-permute-start | bytes 1179656 | tf_op jit(solution)/shard_map/ppermute | solution.py:59
  475.5 18.7 %collective-permute-start.108 = (bf16[3,256,256]{2,1,0:T(8,128)(2,1)S(1)}, bf16[3,256,256]{2,1,0:T(8,128)(2,1)S(1)}, u32[]{:S(2)}, u32[]{:S(2)}) collective-permute-start(bf16[3,256,256]{2,1,0:T(8,128)(2,1)S(1)} %add_convert_fusion.1.refs_0_), channel_id=1, source_target_pairs={{0,12},{4,0},{8,4},{12,8},{1,13},{5,1},{9,5},{13,9},{2,14},{6,2},{... | collective-permute-start | bytes 1179656 | tf_op jit(solution)/shard_map/ppermute | solution.py:59
  (241 other events, 2502.3 us)
